TPU v7x, 128 devices: a whole 4x4x4 slice. The times are simulated.
128 devices in a mesh: region: 64 (over y, x, z), band: 2 (over core).
Axes of the slice: x: 4, y: 4, z: 4, core: 2. Of those that a mesh axis runs over, the one named last changes fastest.
Arguments:
- emission: bfloat16 [65536, 192], P(('region', 'band')), may hold values from 0.099609375 to 10
- path_sends: int32 [128, 128, 64], P(('region', 'band')), may hold values from -1 to 511, as said below
- tile_slots: int32 [1024, 512], P(('region', 'band')), may hold values from -1 to 8191, as said below
- geometry: bfloat16 [1024, 256, 512], P(('region', 'band')), may hold values from 0.00049972534 to 0.0099487305
- absorption: bfloat16 [1024, 8, 512], P(('region', 'band')), may hold values from 0.099609375 to 1
- hour_period: int32 [24], replicated, may hold values from 0 to 2
- dwellings: int32 [262144], P(('region', 'band')), may hold values from 1 to 8
- addr_sends: int32 [128, 128, 16], P(('region', 'band')), may hold values from -1 to 2047, as said below
- addr_building: int32 [128, 128, 16], P(('region', 'band')), may hold values from 0 to 2047
Outputs:
- receiver_level: float32 [262144], P(('region', 'band'))
- building_level: float32 [262144], P(('region', 'band'))
- exposure: float32 [262144, 192], P(('region', 'band'))
Inputs may be any that keep to these rules, and one draw needn't show every extreme that they name: path_sends[s, d, c] is a segment of device s or -1; the live entries of each list come first; some destination gets 64 live entries from every source. tile_slots[t, p] names a received slot s * 64 + c of the tile's device whose entry path_sends[s, d, c] is live, or is -1; live entries of a tile come first, at least 256 of them, and some tile of every device has all 512 live; a slot may feed several paths. addr_sends[s, d, c] is a receiver of device s or -1; live entries of each list come first; each receiver is named at most once over all lists; some destination gets 16 live entries from every source.
All inputs are finite; a program needn't handle non-finite values.
Results may differ from a plain program's by a relative error of at most 0.00034.
Values may be sent and summed in bfloat16 or wider, within the bound.
A program may use at most 64 MiB of HBM per device.

v0:
```python
import math

import jax
import jax.numpy as jnp
from jax import lax
from jax.sharding import PartitionSpec as P

HOURS = 24
BLD_DEV = 2048


A_WEIGHTING_DB = [-26.2, -16.1, -8.6, -3.2, 0.0, 1.2, 1.0, -1.1]


def hour_weights(hour_period):
    a_weight = jnp.power(10.0, jnp.array(A_WEIGHTING_DB, jnp.float32) / 10.0)
    period_gain = jnp.array([1.0, 10.0**0.5, 10.0], jnp.float32)
    matches = hour_period[:, None] == jnp.arange(3, dtype=jnp.int32)[None, :]
    per_hour = jnp.sum(jnp.where(matches, period_gain[None, :], jnp.float32(0.0)), axis=1)
    return (a_weight[:, None] * per_hour[None, :] / HOURS).reshape(-1)


def one_hot_rows(index, extent, kind):
    return (index[:, None] == jnp.arange(extent, dtype=jnp.int32)[None, :]).astype(kind)


def local(
    emission,
    path_sends,
    tile_slots,
    geometry,
    absorption,
    hour_period,
    dwellings,
    addr_sends,
    addr_building,
):
    weights = hour_weights(hour_period)
    width = emission.shape[1]
    seg_count = emission.shape[0]
    send_list = path_sends[0]
    flat_list = send_list.reshape(-1)
    block_rows = math.gcd(flat_list.shape[0], 512)

    def pick_rows(index):
        table = one_hot_rows(index, seg_count, jnp.bfloat16)
        return jnp.dot(table, emission, preferred_element_type=jnp.float32).astype(jnp.bfloat16)

    outgoing = lax.map(pick_rows, flat_list.reshape(-1, block_rows)).reshape(
        send_list.shape + (width,)
    )
    arrived = lax.all_to_all(outgoing, ("region", "band"), split_axis=0, concat_axis=0, tiled=True)
    received = arrived.reshape(-1, width)
    slot_count = received.shape[0]

    def tile_work(items):
        slots, tile_geometry, tile_absorption = items
        table = one_hot_rows(slots, slot_count, jnp.bfloat16)
        gathered = jnp.dot(table, received, preferred_element_type=jnp.float32).astype(jnp.bfloat16)
        factor = jnp.repeat(jnp.swapaxes(tile_absorption, 0, 1), HOURS, axis=1)
        mixed_rows = (factor.astype(jnp.float32) * gathered.astype(jnp.float32)).astype(
            jnp.bfloat16
        )
        return jnp.dot(tile_geometry, mixed_rows, preferred_element_type=jnp.float32)

    exposure = lax.map(tile_work, (tile_slots, geometry, absorption))
    flat_rows = exposure.reshape(-1, width)
    levels = jnp.log10(jnp.dot(flat_rows, weights, precision=lax.Precision.HIGHEST))
    address_list = addr_sends[0]
    recv_count = flat_rows.shape[0]
    select = one_hot_rows(address_list.reshape(-1), recv_count, jnp.float32)
    dwell_weight = jnp.dot(
        select, dwellings.astype(jnp.float32), precision=lax.Precision.HIGHEST
    ).reshape(address_list.shape)
    level_at = jnp.dot(select, levels, precision=lax.Precision.HIGHEST).reshape(address_list.shape)
    weighted_out = dwell_weight * level_at
    weighted_in, dwell_in = (
        lax.all_to_all(weighted_out, ("region", "band"), split_axis=0, concat_axis=0, tiled=True),
        lax.all_to_all(dwell_weight, ("region", "band"), split_axis=0, concat_axis=0, tiled=True),
    )
    building = addr_building[0].reshape(-1)
    owner_table = (jnp.arange(BLD_DEV, dtype=jnp.int32)[:, None] == building[None, :]).astype(
        jnp.float32
    )
    numerator = jnp.dot(owner_table, weighted_in.reshape(-1), precision=lax.Precision.HIGHEST)
    denominator = jnp.dot(owner_table, dwell_in.reshape(-1), precision=lax.Precision.HIGHEST)
    return (levels, numerator / jnp.maximum(denominator, jnp.float32(1.0)), flat_rows)


def solution(mesh):
    in_specs = (
        P(("region", "band"), None),
        P(("region", "band"), None, None),
        P(("region", "band"), None),
        P(("region", "band"), None, None),
        P(("region", "band"), None, None),
        P(),
        P(("region", "band")),
        P(("region", "band"), None, None),
        P(("region", "band"), None, None),
    )
    out_specs = (P(("region", "band")), P(("region", "band")), P(("region", "band"), None))
    return jax.shard_map(local, mesh=mesh, in_specs=in_specs, out_specs=out_specs, check_vma=False)
```

profile of v0, /device:TPU:1, one launch (start us, length us, event | category | flops | bytes accessed | tf_op | source)
XLA Modules:
  0.0 216.4 jit_solution(1910211945657478047)
XLA Ops:
  2.3 7.5 %fusion.13 = f32[1,2048]{1,0:T(1,128)S(1)} fusion(f32[2048,1]{0,1:T(1,128)S(1)} %bitcast.73, s32[2048]{0:T(1024)S(1)} %eq.80), kind=kOutput, calls=%fused_computation.21 | convolution fusion | flops 54525952 | bytes 24576 | tf_op jit(solution)/shard_map/dot_general | solution.py:72
  10.5 11.5 %all-to-all-start.2 = ((f32[128,1,16]{2,1,0:T(1,128)}), f32[128,1,16]{2,1,0:T(1,128)S(1)}, u32[]{:S(2)}, u32[]{:S(2)}) async-start(f32[128,1,16]{2,1,0:T(1,128)} %bitcast.17), calls=%async_computation.2 | async-start | bytes 131072 | tf_op jit(solution)/shard_map/all_to_all | solution.py:79
  22.2 8.1 %while.20 = (s32[]{:T(128)}, bf16[16,512,192]{1,2,0:T(8,128)(2,1)S(1)}, s32[16,512]{1,0:T(8,128)S(1)}, bf16[512,192]{0,1:T(8,128)(2,1)S(1)}, s32[]{:T(128)}) while((s32[]{:T(128)}, bf16[16,512,192]{1,2,0:T(8,128)(2,1)S(1)}, s32[16,512]{1,0:T(8,128)S(1)}, bf16[512,192]{0,1:T(8,128)(2,1)S(1)}, s32[]{:T(128)}) %tuple.41), condition=%wide.region_1.2_spmd, body=%wide.region_0.1_spmd.sunk | while | flops 101023744 | bytes 399429 | solution.py:49
  30.3 4.0 %copy.30 = bf16[16,512,192]{2,1,0:T(8,128)(2,1)} copy(bf16[16,512,192]{1,2,0:T(8,128)(2,1)S(1)} %get-tuple-element.57) | data formatting | bytes 6291456 | tf_op jit(solution)/shard_map/while | solution.py:49
  34.4 10.2 %all-to-all-start = ((bf16[128,64,192]{2,1,0:T(8,128)(2,1)}), bf16[128,64,192]{2,1,0:T(8,128)(2,1)}, u32[]{:S(2)}, u32[]{:S(2)}) async-start(bf16[128,64,192]{2,1,0:T(8,128)(2,1)} %bitcast.60), calls=%async_computation | async-start | bytes 8388608 | tf_op jit(solution)/shard_map/all_to_all | solution.py:52
  46.4 50.8 %all-to-all-done = bf16[128,64,192]{2,1,0:T(8,128)(2,1)} async-done(((bf16[128,64,192]{2,1,0:T(8,128)(2,1)}), bf16[128,64,192]{2,1,0:T(8,128)(2,1)}, u32[]{:S(2)}, u32[]{:S(2)}) %all-to-all-start) | async-done | bytes 3145760 | tf_op jit(solution)/shard_map/all_to_all | solution.py:52
  97.2 85.7 %while.21 = (s32[]{:T(128)}, f32[8,256,192]{1,0,2:T(8,128)S(1)}, bf16[8,256,512]{2,1,0:T(8,128)(2,1)}, bf16[8,8,512]{2,1,0:T(8,128)(2,1)}, s32[8,512]{1,0:T(8,12...) while((s32[]{:T(128)}, f32[8,256,192]{1,0,2:T(8,128)S(1)}, bf16[8,256,512]{2,1,0:T(8,128)(2,1)}, ...), condition=%wide.region_3.4_spmd, body=%wide.region_2.3_spmd.sunk | while | flops 1665536000 | bytes 6273633 | solution.py:66
  98.7 6.4 %convolution_bitcast_fusion.2 = f32[1,256,192]{1,2,0:T(8,128)S(1)} fusion(f32[512,192]{0,1:T(8,128)S(1)} %bitcast.61, bf16[8192,192]{1,0:T(8,128)(2,1)} %get-tuple-element.177, s32[512]{0:T(512)S(1)} %bitcast.66, bf16[8,256,512]{2,1,0:T(8,128)(2,1)} %get-tuple-element.174, s32[]{:T(128)} %get-tuple-element.164), kind=kOutput, calls=%fused_computation.13.clone.1 | convolution fusion | flops 1665531904 | bytes 5048832 | tf_op jit(solution)/shard_map/while/body/eval_jaxpr/dot_general | solution.py:64
  105.3 2.6 %dynamic_update_slice.12 = f32[8,256,192]{1,0,2:T(8,128)S(1)} dynamic-update-slice(f32[8,256,192]{1,0,2:T(8,128)S(1)} %get-tuple-element.165, f32[1,256,192]{1,0,2:T(1,128)S(1)} %copy.41, s32[]{:T(128)} %get-tuple-element.164, s32[]{:T(128)} %constant.21.clone.1..sunk, s32[]{:T(128)} %constant.21.clone.1..sunk) | dynamic-update-slice | bytes 393220 | tf_op jit(solution)/shard_map/while/body/jit(dynamic_update_index_in_dim)/dynamic_update_slice | solution.py:66
  109.4 6.4 %convolution_bitcast_fusion.2 = f32[1,256,192]{1,2,0:T(8,128)S(1)} fusion(f32[512,192]{0,1:T(8,128)S(1)} %bitcast.61, bf16[8192,192]{1,0:T(8,128)(2,1)} %get-tuple-element.177, s32[512]{0:T(512)S(1)} %bitcast.66, bf16[8,256,512]{2,1,0:T(8,128)(2,1)} %get-tuple-element.174, s32[]{:T(128)} %get-tuple-element.164), kind=kOutput, calls=%fused_computation.13.clone.1 | convolution fusion | flops 1665531904 | bytes 5048832 | tf_op jit(solution)/shard_map/while/body/eval_jaxpr/dot_general | solution.py:64
  116.0 2.6 %dynamic_update_slice.12 = f32[8,256,192]{1,0,2:T(8,128)S(1)} dynamic-update-slice(f32[8,256,192]{1,0,2:T(8,128)S(1)} %get-tuple-element.165, f32[1,256,192]{1,0,2:T(1,128)S(1)} %copy.41, s32[]{:T(128)} %get-tuple-element.164, s32[]{:T(128)} %constant.21.clone.1..sunk, s32[]{:T(128)} %constant.21.clone.1..sunk) | dynamic-update-slice | bytes 393220 | tf_op jit(solution)/shard_map/while/body/jit(dynamic_update_index_in_dim)/dynamic_update_slice | solution.py:66
  120.1 6.4 %convolution_bitcast_fusion.2 = f32[1,256,192]{1,2,0:T(8,128)S(1)} fusion(f32[512,192]{0,1:T(8,128)S(1)} %bitcast.61, bf16[8192,192]{1,0:T(8,128)(2,1)} %get-tuple-element.177, s32[512]{0:T(512)S(1)} %bitcast.66, bf16[8,256,512]{2,1,0:T(8,128)(2,1)} %get-tuple-element.174, s32[]{:T(128)} %get-tuple-element.164), kind=kOutput, calls=%fused_computation.13.clone.1 | convolution fusion | flops 1665531904 | bytes 5048832 | tf_op jit(solution)/shard_map/while/body/eval_jaxpr/dot_general | solution.py:64
  126.7 2.6 %dynamic_update_slice.12 = f32[8,256,192]{1,0,2:T(8,128)S(1)} dynamic-update-slice(f32[8,256,192]{1,0,2:T(8,128)S(1)} %get-tuple-element.165, f32[1,256,192]{1,0,2:T(1,128)S(1)} %copy.41, s32[]{:T(128)} %get-tuple-element.164, s32[]{:T(128)} %constant.21.clone.1..sunk, s32[]{:T(128)} %constant.21.clone.1..sunk) | dynamic-update-slice | bytes 393220 | tf_op jit(solution)/shard_map/while/body/jit(dynamic_update_index_in_dim)/dynamic_update_slice | solution.py:66
  130.7 6.4 %convolution_bitcast_fusion.2 = f32[1,256,192]{1,2,0:T(8,128)S(1)} fusion(f32[512,192]{0,1:T(8,128)S(1)} %bitcast.61, bf16[8192,192]{1,0:T(8,128)(2,1)} %get-tuple-element.177, s32[512]{0:T(512)S(1)} %bitcast.66, bf16[8,256,512]{2,1,0:T(8,128)(2,1)} %get-tuple-element.174, s32[]{:T(128)} %get-tuple-element.164), kind=kOutput, calls=%fused_computation.13.clone.1 | convolution fusion | flops 1665531904 | bytes 5048832 | tf_op jit(solution)/shard_map/while/body/eval_jaxpr/dot_general | solution.py:64
  137.4 2.6 %dynamic_update_slice.12 = f32[8,256,192]{1,0,2:T(8,128)S(1)} dynamic-update-slice(f32[8,256,192]{1,0,2:T(8,128)S(1)} %get-tuple-element.165, f32[1,256,192]{1,0,2:T(1,128)S(1)} %copy.41, s32[]{:T(128)} %get-tuple-element.164, s32[]{:T(128)} %constant.21.clone.1..sunk, s32[]{:T(128)} %constant.21.clone.1..sunk) | dynamic-update-slice | bytes 393220 | tf_op jit(solution)/shard_map/while/body/jit(dynamic_update_index_in_dim)/dynamic_update_slice | solution.py:66
  141.4 6.4 %convolution_bitcast_fusion.2 = f32[1,256,192]{1,2,0:T(8,128)S(1)} fusion(f32[512,192]{0,1:T(8,128)S(1)} %bitcast.61, bf16[8192,192]{1,0:T(8,128)(2,1)} %get-tuple-element.177, s32[512]{0:T(512)S(1)} %bitcast.66, bf16[8,256,512]{2,1,0:T(8,128)(2,1)} %get-tuple-element.174, s32[]{:T(128)} %get-tuple-element.164), kind=kOutput, calls=%fused_computation.13.clone.1 | convolution fusion | flops 1665531904 | bytes 5048832 | tf_op jit(solution)/shard_map/while/body/eval_jaxpr/dot_general | solution.py:64
  148.1 2.6 %dynamic_update_slice.12 = f32[8,256,192]{1,0,2:T(8,128)S(1)} dynamic-update-slice(f32[8,256,192]{1,0,2:T(8,128)S(1)} %get-tuple-element.165, f32[1,256,192]{1,0,2:T(1,128)S(1)} %copy.41, s32[]{:T(128)} %get-tuple-element.164, s32[]{:T(128)} %constant.21.clone.1..sunk, s32[]{:T(128)} %constant.21.clone.1..sunk) | dynamic-update-slice | bytes 393220 | tf_op jit(solution)/shard_map/while/body/jit(dynamic_update_index_in_dim)/dynamic_update_slice | solution.py:66
  152.1 6.4 %convolution_bitcast_fusion.2 = f32[1,256,192]{1,2,0:T(8,128)S(1)} fusion(f32[512,192]{0,1:T(8,128)S(1)} %bitcast.61, bf16[8192,192]{1,0:T(8,128)(2,1)} %get-tuple-element.177, s32[512]{0:T(512)S(1)} %bitcast.66, bf16[8,256,512]{2,1,0:T(8,128)(2,1)} %get-tuple-element.174, s32[]{:T(128)} %get-tuple-element.164), kind=kOutput, calls=%fused_computation.13.clone.1 | convolution fusion | flops 1665531904 | bytes 5048832 | tf_op jit(solution)/shard_map/while/body/eval_jaxpr/dot_general | solution.py:64
  162.8 6.4 %convolution_bitcast_fusion.2 = f32[1,256,192]{1,2,0:T(8,128)S(1)} fusion(f32[512,192]{0,1:T(8,128)S(1)} %bitcast.61, bf16[8192,192]{1,0:T(8,128)(2,1)} %get-tuple-element.177, s32[512]{0:T(512)S(1)} %bitcast.66, bf16[8,256,512]{2,1,0:T(8,128)(2,1)} %get-tuple-element.174, s32[]{:T(128)} %get-tuple-element.164), kind=kOutput, calls=%fused_computation.13.clone.1 | convolution fusion | flops 1665531904 | bytes 5048832 | tf_op jit(solution)/shard_map/while/body/eval_jaxpr/dot_general | solution.py:64
  173.5 6.4 %convolution_bitcast_fusion.2 = f32[1,256,192]{1,2,0:T(8,128)S(1)} fusion(f32[512,192]{0,1:T(8,128)S(1)} %bitcast.61, bf16[8192,192]{1,0:T(8,128)(2,1)} %get-tuple-element.177, s32[512]{0:T(512)S(1)} %bitcast.66, bf16[8,256,512]{2,1,0:T(8,128)(2,1)} %get-tuple-element.174, s32[]{:T(128)} %get-tuple-element.164), kind=kOutput, calls=%fused_computation.13.clone.1 | convolution fusion | flops 1665531904 | bytes 5048832 | tf_op jit(solution)/shard_map/while/body/eval_jaxpr/dot_general | solution.py:64
  184.5 7.5 %fusion.12 = f32[1,2048]{1,0:T(1,128)S(1)} fusion(f32[2048,1]{0,1:T(1,128)S(1)} %bitcast.72, s32[2048]{0:T(1024)S(1)} %eq.80), kind=kOutput, calls=%fused_computation.20 | convolution fusion | flops 54525952 | bytes 24576 | tf_op jit(solution)/shard_map/dot_general | solution.py:75
  193.6 4.5 %all-to-all-start.1 = ((f32[128,1,16]{2,1,0:T(1,128)}), f32[128,1,16]{2,1,0:T(1,128)S(1)}, u32[]{:S(2)}, u32[]{:S(2)}) async-start(f32[128,1,16]{2,1,0:T(1,128)} %bitcast.15), calls=%async_computation.1 | async-start | bytes 131072 | tf_op jit(solution)/shard_map/all_to_all | solution.py:78
  198.1 7.4 %fusion.14 = f32[1,2048]{1,0:T(1,128)S(1)} fusion(f32[2048,1]{0,1:T(1,128)S(1)} %reshape.94, s32[2048]{0:T(1024)S(1)} %eq.77), kind=kOutput, calls=%fused_computation.23 | convolution fusion | flops 54525952 | bytes 24576 | tf_op jit(solution)/shard_map/dot_general | solution.py:86
  208.4 7.4 %fusion.15 = f32[1,2048]{1,0:T(1,128)S(1)} fusion(f32[2048,1]{0,1:T(1,128)S(1)} %reshape.92, s32[2048]{0:T(1024)S(1)} %eq.77), kind=kOutput, calls=%fused_computation.24 | convolution fusion | flops 54525952 | bytes 24576 | tf_op jit(solution)/shard_map/dot_general | solution.py:85
  (109 shorter events, 39.6 us)
Async XLA Ops:
  0.6 21.4 %copy-start.1 = (s32[1,128,64]{1,2,0:T(8,128)S(1)}, s32[1,128,64]{1,2,0:T(8,128)}, u32[]{:S(2)}) copy-start(s32[1,128,64]{1,2,0:T(8,128)} %param.16) | copy-start | bytes 98308
  0.6 21.6 %copy-start.5 = (bf16[512,192]{0,1:T(8,128)(2,1)S(1)}, bf16[512,192]{0,1:T(8,128)(2,1)}, u32[]{:S(2)}) copy-start(bf16[512,192]{0,1:T(8,128)(2,1)} %param.15) | copy-start | bytes 589828
  10.5 23.8 %all-to-all-start.2 = ((f32[128,1,16]{2,1,0:T(1,128)}), f32[128,1,16]{2,1,0:T(1,128)S(1)}, u32[]{:S(2)}, u32[]{:S(2)}) async-start(f32[128,1,16]{2,1,0:T(1,128)} %bitcast.17), calls=%async_computation.2 | async-start | bytes 131072 | tf_op jit(solution)/shard_map/all_to_all | solution.py:79
  34.3 10.3 %copy-start.6 = (s32[24]{0:T(128)S(1)}, s32[24]{0:T(128)}, u32[]{:S(2)}) copy-start(s32[24]{0:T(128)} %param.20) | copy-start | bytes 292
  34.3 10.3 %copy-start.7 = (f32[3]{0:T(128)S(1)}, f32[3]{0:T(128)}, u32[]{:S(2)}) copy-start(f32[3]{0:T(128)} %constant.45.clone) | copy-start | bytes 40
  34.3 10.4 %copy-start.4 = (f32[8]{0:T(128)S(1)}, f32[8]{0:T(128)}, u32[]{:S(2)}) copy-start(f32[8]{0:T(128)} %constant.53) | copy-start | bytes 100
  34.4 10.5 %copy-start.2 = (s32[1,128,16]{1,2,0:T(8,128)S(1)}, s32[1,128,16]{1,2,0:T(8,128)}, u32[]{:S(2)}) copy-start(s32[1,128,16]{1,2,0:T(8,128)} %param.23) | copy-start | bytes 24580
  34.4 62.8 %all-to-all-start = ((bf16[128,64,192]{2,1,0:T(8,128)(2,1)}), bf16[128,64,192]{2,1,0:T(8,128)(2,1)}, u32[]{:S(2)}, u32[]{:S(2)}) async-start(bf16[128,64,192]{2,1,0:T(8,128)(2,1)} %bitcast.60), calls=%async_computation | async-start | bytes 8388608 | tf_op jit(solution)/shard_map/all_to_all | solution.py:52
  183.5 22.0 %copy-start = (f32[24,8,8,256]{3,1,2,0:T(8,128)}, f32[24,8,8,256]{3,1,2,0:T(8,128)S(1)}, u32[]{:S(2)}) copy-start(f32[24,8,8,256]{3,1,2,0:T(8,128)S(1)} %copy.39) | copy-start | bytes 4718596
  184.5 21.0 %copy-start.3 = (f32[2048]{0:T(1024)}, f32[2048]{0:T(1024)S(1)}, u32[]{:S(2)}) copy-start(f32[2048]{0:T(1024)S(1)} %log_multiply_fusion) | copy-start | bytes 24580
  193.6 14.0 %all-to-all-start.1 = ((f32[128,1,16]{2,1,0:T(1,128)}), f32[128,1,16]{2,1,0:T(1,128)S(1)}, u32[]{:S(2)}, u32[]{:S(2)}) async-start(f32[128,1,16]{2,1,0:T(1,128)} %bitcast.15), calls=%async_computation.1 | async-start | bytes 131072 | tf_op jit(solution)/shard_map/all_to_all | solution.py:78
where the time goes:
time: 218 us; the launch traced here: 216 us
  matrix products  89.5 us (41%)
  waiting for transfers between devices  52.8 us (24%)
  local copies, waits for them, and re-layouts  36 us (17%)
  starting transfers between devices  26.2 us (12%)
  other arithmetic  10 us (5%)
    dot_general x8, matrix products, tile_work(): jnp.dot(tile_geometry, mixed_rows, preferred_element_type=jnp.float32)  51.3 us
    all_to_all x1, waiting for transfers between devices, local(): lax.all_to_all(outgoing, ('region', 'band'), split_axis=0, concat_axis=0,...  50.8 us
    dynamic_update_slice x16, local copies, waits for them, and re-layouts, local(): exposure = lax.map(tile_work, (tile_slots, geometry, absorption))  22.2 us
    all_to_all x1, starting transfers between devices, local(): lax.all_to_all(dwell_weight, ('region', 'band'), split_axis=0, concat_axi...  11.5 us
    all_to_all x1, starting transfers between devices, local(): lax.all_to_all(outgoing, ('region', 'band'), split_axis=0, concat_axis=0,...  10.2 us
    dot_general x1, matrix products, local(): jnp.dot(select, levels, precision=lax.Precision.HIGHEST)  7.52 us
    dot_general x1, matrix products, local(): jnp.dot(select, dwellings.astype(jnp.float32), precision=lax.Precision.HI...  7.52 us
    dot_general x16, matrix products, pick_rows(): jnp.dot(table, emission, preferred_element_type=jnp.float32)  7.48 us
  transfers between devices with their start and end apart: 3, of which 2 were waited for; matrix products, arithmetic and copies ran while one was open for 10% of the time, Pallas kernels for 0%

commit v1 on v0

v1 whole, which is shorter than its diff:
```python
import math

import jax
import jax.numpy as jnp
from jax import lax
from jax.experimental import pallas as pl
from jax.experimental.pallas import tpu as pltpu
from jax.sharding import PartitionSpec as P

BANDS = 8
HOURS = 24
WIDTH = BANDS * HOURS
SEG_DEV = 512
CAP = 64
TILE_DEV = 8
RECV_TILE = 256
PATHS_TILE = 512
CAP_ADDR = 16
DEVICES = 128
PATHS = TILE_DEV * PATHS_TILE
BLOCK = 96
MIX, UNMIX = 45, 37
GROUP = 16
PICK = 4
A_WEIGHTING_DB = (-26.2, -16.1, -8.6, -3.2, 0.0, 1.2, 1.0, -1.1)
MESH = pl.DeviceIdType.MESH
BF16, F32, I32 = jnp.bfloat16, jnp.float32, jnp.int32


def my_place():
    region, core = lax.axis_index("region"), lax.axis_index("band")
    return region // 16, (region // 4) % 4, region % 4, core


def peer(step):
    y, x, z, core = my_place()
    shift = (step * MIX) % DEVICES
    region = ((y + shift // 32) % 4) * 16 + ((x + (shift // 8) % 4) % 4) * 4 + (z + (shift // 2) % 4) % 4
    return region, (core + shift) % 2


def step_of_source(source):
    y, x, z, core = my_place()
    dy = (y + 4 - source // 32) % 4
    dx = (x + 4 - (source // 8) % 4) % 4
    dz = (z + 4 - (source // 2) % 4) % 4
    dc = (core + 2 - source % 2) % 2
    return ((dy * 32 + dx * 8 + dz * 2 + dc) * UNMIX) % DEVICES


def split3(value):
    high = value.astype(BF16)
    rest = value - high.astype(F32)
    mid = rest.astype(BF16)
    return high, mid, (rest - mid.astype(F32)).astype(BF16)


def kernel(
    em_ref, ps_ref, slot_ref, geo_hbm, abs_ref, hour_ref, dwell_ref, addr_ref, bld_ref,
    level_ref, build_ref, expo_ref,
    rows, outb, recv, rhs, acc, hi_ref, lo_ref, geo, weight, msg_out, msg_in,
    geo_sem, self_sem, send_sem, recv_sem, msend_sem, mrecv_sem,
):
    region, core = lax.axis_index("region"), lax.axis_index("band")
    me = region * 2 + core
    geo_copy = pltpu.make_async_copy(geo_hbm, geo, geo_sem)
    geo_copy.start()
    barrier = pltpu.get_barrier_semaphore()

    def greet(step, carry):
        pl.semaphore_signal(barrier, inc=1, device_id=peer(step), device_id_type=MESH)
        return carry

    lax.fori_loop(1, DEVICES, greet, 0)

    em = em_ref[...].astype(F32)
    rows[...] = jnp.concatenate([em, em[128:192]], axis=0).T.astype(BF16)
    lists = ps_ref[...].astype(F32)
    low_lanes = lax.broadcasted_iota(I32, (32, 128), 1) < 64

    def pick(group):
        columns = []
        for u in range(PICK):
            to_region, to_core = peer(group * PICK + u)
            dest = to_region * 2 + to_core
            hit = lax.broadcasted_iota(I32, (CAP, DEVICES), 1) == dest
            columns.append(jnp.sum(jnp.where(hit, lists, 0.0), axis=1, keepdims=True))
        column = jnp.concatenate(columns, axis=0)
        lane = lax.broadcasted_iota(I32, (PICK * CAP, SEG_DEV), 1).astype(F32)
        table = jnp.where(lane == column, 1.0, 0.0).astype(BF16)
        picked = jnp.dot(table, rows[...], preferred_element_type=F32).astype(BF16)
        for u in range(PICK):
            step = group * PICK + u
            block = picked[u * CAP : (u + 1) * CAP]
            outb[step, 0:64, :] = block[:, 0:128]
            outb[step, 64:96, :] = jnp.where(low_lanes, block[0:32, 128:256], block[32:64, 128:256])

    def send(step):
        pltpu.make_async_remote_copy(
            src_ref=outb.at[step], dst_ref=recv.at[step], send_sem=send_sem, recv_sem=recv_sem.at[step // GROUP],
            device_id=peer(step), device_id_type=MESH,
        ).start()

    pick(0)
    pl.semaphore_wait(barrier, DEVICES - 1)
    own_copy = pltpu.make_async_copy(outb.at[0], recv.at[0], self_sem)
    own_copy.start()
    for u in range(1, PICK):
        send(u)

    def pick_and_send(group, carry):
        pick(group)
        for u in range(PICK):
            send(group * PICK + u)
        return carry

    lax.fori_loop(1, DEVICES // PICK, pick_and_send, 0)

    slots = slot_ref[...]
    safe = jnp.maximum(slots, 0)
    place = step_of_source(safe // CAP) * CAP + safe % CAP
    label = jnp.where(slots >= 0, place, -1)
    high = (label // 256).astype(F32)
    low = (label % 256).astype(F32)
    high = jnp.where(slots >= 0, high, -1.0)
    for t in range(TILE_DEV):
        for q in range(PATHS_TILE // 128):
            at = pl.ds(t * PATHS_TILE + q * 128, 128)
            cols = slice(q * 128, (q + 1) * 128)
            hi_ref[at, :] = jnp.broadcast_to(high[t : t + 1, cols], (128, 128)).T.astype(BF16)
            lo_ref[at, :] = jnp.broadcast_to(low[t : t + 1, cols], (128, 128)).T.astype(BF16)

    r = lax.broadcasted_iota(I32, (WIDTH, 128), 0)
    scale = jnp.zeros((WIDTH, 128), F32)
    for b in range(BANDS):
        scale = jnp.where(r // HOURS == b, jnp.float32(10.0 ** (A_WEIGHTING_DB[b] / 10.0)), scale)
    gain = jnp.zeros((WIDTH, 128), F32)
    for h in range(HOURS):
        period = hour_ref[h]
        g = jnp.where(period == 0, 1.0, jnp.where(period == 1, jnp.float32(10.0**0.5), jnp.where(period == 2, 10.0, 0.0)))
        gain = jnp.where(r % HOURS == h, g.astype(F32), gain)
    weight[...] = scale * gain / HOURS

    acc[...] = jnp.zeros_like(acc)
    ROWS = 1024

    def gather(group, carry):
        blocks = recv[pl.ds(group * GROUP, GROUP)]
        main = blocks[:, 0:64, :].reshape(GROUP * CAP, 128)
        side = blocks[:, 64:96, :]
        rhs[:, 0:128] = main
        rhs[:, 128:256] = jnp.concatenate([side, side], axis=1).reshape(GROUP * CAP, 128)

        def some_paths(i, inner):
            at = pl.ds(pl.multiple_of(i * ROWS, ROWS), ROWS)
            lo, hi = lo_ref[at, :], hi_ref[at, :]
            parts = []
            for u in range(GROUP * CAP // 256):
                here = (group * (GROUP * CAP // 256) + u).astype(F32).astype(BF16)
                own = jnp.where(hi == here, lo, BF16(-1))
                for half in range(2):
                    lane = (lax.broadcasted_iota(I32, (ROWS, 128), 1) + half * 128).astype(F32).astype(BF16)
                    parts.append(jnp.where(own == lane, BF16(1), BF16(0)))
            table = jnp.concatenate(parts, axis=1)
            acc[at, :] = acc[at, :] + jnp.dot(table, rhs[...], preferred_element_type=F32)
            return inner

        lax.fori_loop(0, PATHS // ROWS, some_paths, 0)
        return carry

    def arrived(group):
        ref = recv.at[pl.ds(group * GROUP, GROUP)]
        return pltpu.make_async_copy(ref, ref, recv_sem.at[group])

    own_copy.wait()
    first = recv.at[pl.ds(1, GROUP - 1)]
    pltpu.make_async_copy(first, first, recv_sem.at[0]).wait()
    gather(jnp.int32(0), 0)

    def wait_and_gather(group, carry):
        arrived(group).wait()
        return gather(group, carry)

    lax.fori_loop(1, DEVICES // GROUP, wait_and_gather, 0)
    geo_copy.wait()

    def tile(t, carry):
        table = acc[pl.ds(pl.multiple_of(t * PATHS_TILE, PATHS_TILE), PATHS_TILE), :].T
        first_half = slot_ref[pl.ds(t, 1), :] % CAP < 32
        tail = jnp.where(first_half, table[128:192], table[192:256])
        gathered = jnp.concatenate([table[0:128], tail], axis=0)
        damp = abs_ref[t].astype(F32)
        factor = jnp.concatenate(
            [jnp.broadcast_to(damp[b : b + 1], (HOURS, PATHS_TILE)) for b in range(BANDS)], axis=0
        )
        mixed = (factor * gathered).astype(BF16)
        exposure = lax.dot_general(mixed, geo[t], (((1,), (1,)), ((), ())), preferred_element_type=F32)
        expo_ref[:, pl.ds(pl.multiple_of(t * RECV_TILE, RECV_TILE), RECV_TILE)] = exposure
        for half in range(2):
            energy = jnp.sum(exposure[:, half * 128 : (half + 1) * 128] * weight[...], axis=0, keepdims=True)
            level_ref[pl.ds(2 * t + half, 1), :] = jnp.log(energy) * jnp.float32(1.0 / math.log(10.0))
        return carry

    lax.fori_loop(0, TILE_DEV, tile, 0)

    dwell = dwell_ref[...].astype(F32)
    table = jnp.concatenate([*split3(dwell * level_ref[...]), dwell.astype(BF16)], axis=0)
    addr = addr_ref[...]
    addr_high, addr_low = jnp.maximum(addr, 0) // 128, jnp.where(addr >= 0, addr % 128, -1)
    sub = lax.broadcasted_iota(I32, (128, 128), 0)
    weighted, dwelt = [], []
    for c in range(CAP_ADDR):
        hot = jnp.where(sub == addr_low[c : c + 1], 1.0, 0.0).astype(BF16)
        found = jnp.dot(table, hot, preferred_element_type=F32)
        level_rows = found[0:16] + found[16:32] + found[32:48]
        mine = lax.broadcasted_iota(I32, (16, 128), 0) == addr_high[c : c + 1]
        weighted.append(jnp.sum(jnp.where(mine, level_rows, 0.0), axis=0, keepdims=True))
        dwelt.append(jnp.sum(jnp.where(mine, found[48:64], 0.0), axis=0, keepdims=True))
    message = jnp.concatenate(weighted + dwelt + [jnp.zeros((96, 128), F32)], axis=0).T
    msg_out[:, 0, :] = message
    msg_in[pl.ds(me, 1)] = msg_out[pl.ds(me, 1)]

    def post(step, carry):
        to_region, to_core = peer(step)
        pltpu.make_async_remote_copy(
            src_ref=msg_out.at[to_region * 2 + to_core], dst_ref=msg_in.at[me], send_sem=msend_sem, recv_sem=mrecv_sem,
            device_id=(to_region, to_core), device_id_type=MESH,
        ).start()
        return carry

    lax.fori_loop(1, DEVICES, post, 0)
    all_in = msg_in.at[pl.ds(0, DEVICES - 1)]
    pltpu.make_async_copy(all_in, all_in, mrecv_sem).wait()

    got = msg_in[:, 0, :].T
    bld = bld_ref[...]
    bld_high, bld_low = bld // 128, bld % 128
    lhs, hots = [], []
    for c in range(CAP_ADDR):
        mine = lax.broadcasted_iota(I32, (16, 128), 0) == bld_high[c : c + 1]
        spread = jnp.where(mine, got[c : c + 1], 0.0)
        count = jnp.where(mine, got[16 + c : 17 + c], 0.0)
        lhs.append(jnp.concatenate([*split3(spread), count.astype(BF16)], axis=0))
        hots.append(jnp.where(sub == bld_low[c : c + 1], 1.0, 0.0).astype(BF16))
    sums = lax.dot_general(
        jnp.concatenate(lhs, axis=1), jnp.concatenate(hots, axis=1), (((1,), (1,)), ((), ())), preferred_element_type=F32
    )
    build_ref[...] = (sums[0:16] + sums[16:32] + sums[32:48]) / jnp.maximum(sums[48:64], 1.0)

    all_out = outb.at[pl.ds(0, DEVICES - 1)]
    pltpu.make_async_copy(all_out, all_out, send_sem).wait()
    all_mail = msg_out.at[pl.ds(0, DEVICES - 1)]
    pltpu.make_async_copy(all_mail, all_mail, msend_sem).wait()


def local(emission, path_sends, tile_slots, geometry, absorption, hour_period, dwellings, addr_sends, addr_building):
    vmem = pl.BlockSpec(memory_space=pltpu.VMEM)
    level, building, exposure = pl.pallas_call(
        kernel,
        out_shape=(
            jax.ShapeDtypeStruct((16, 128), F32),
            jax.ShapeDtypeStruct((16, 128), F32),
            jax.ShapeDtypeStruct((WIDTH, TILE_DEV * RECV_TILE), F32),
        ),
        in_specs=[vmem, vmem, vmem, pl.BlockSpec(memory_space=pl.ANY), vmem, pl.BlockSpec(memory_space=pltpu.SMEM), vmem, vmem, vmem],
        out_specs=(vmem, vmem, vmem),
        scratch_shapes=[
            pltpu.VMEM((SEG_DEV, 256), BF16),
            pltpu.VMEM((DEVICES, BLOCK, 128), BF16),
            pltpu.VMEM((DEVICES, BLOCK, 128), BF16),
            pltpu.VMEM((GROUP * CAP, 256), BF16),
            pltpu.VMEM((PATHS, 256), F32),
            pltpu.VMEM((PATHS, 128), BF16),
            pltpu.VMEM((PATHS, 128), BF16),
            pltpu.VMEM((TILE_DEV, RECV_TILE, PATHS_TILE), BF16),
            pltpu.VMEM((WIDTH, 128), F32),
            pltpu.VMEM((DEVICES, 1, 128), F32),
            pltpu.VMEM((DEVICES, 1, 128), F32),
            pltpu.SemaphoreType.DMA,
            pltpu.SemaphoreType.DMA,
            pltpu.SemaphoreType.DMA,
            pltpu.SemaphoreType.DMA((DEVICES // GROUP,)),
            pltpu.SemaphoreType.DMA,
            pltpu.SemaphoreType.DMA,
        ],
        compiler_params=pltpu.CompilerParams(collective_id=0, has_side_effects=True, vmem_limit_bytes=56 * 2**20),
        name="noise_map",
    )(
        emission.T,
        path_sends[0].T,
        tile_slots,
        geometry,
        absorption,
        hour_period,
        dwellings.reshape(16, 128),
        addr_sends[0].T,
        addr_building[0].T,
    )
    return level.reshape(-1), building.reshape(-1), exposure.T


def solution(mesh):
    both = ("region", "band")
    in_specs = (P(both, None), P(both, None, None), P(both, None), P(both, None, None), P(both, None, None), P(), P(both), P(both, None, None), P(both, None, None))
    out_specs = (P(both), P(both), P(both, None))
    return jax.shard_map(local, mesh=mesh, in_specs=in_specs, out_specs=out_specs, check_vma=False)
```

time: 218 us -> 88.4 us (0.41)
  matrix products: 89.5 us -> 0 us
  Pallas kernels: 0 us -> 81.4 us
  waiting for transfers between devices: 52.8 us -> 0 us
  local copies, waits for them, and re-layouts: 36 us -> 5.29 us
  starting transfers between devices: 26.2 us -> 0 us
  other arithmetic: 10 us -> 0 us
    dot_general x29 -> x0, matrix products: 89.5 us -> none  [the longest x8 51.3 us: tile_work(): jnp.dot(tile_geometry, mixed_rows, preferred_element_type=jnp.float32)]
    pallas_call x0 -> x1, Pallas kernels: none -> 81.4 us  [local(): pl.pallas_call(kernel, out_shape=(jax.ShapeDtypeStruct((16, 128), F32), j...]
    all_to_all x3 -> x0, waiting for transfers between devices: 52.8 us -> none  [the longest x1 50.8 us: local(): lax.all_to_all(outgoing, ('region', 'band'), split_axis=0, concat_axis=0,...]
    all_to_all x3 -> x0, starting transfers between devices: 26.2 us -> none  [the longest x1 11.5 us: local(): lax.all_to_all(dwell_weight, ('region', 'band'), split_axis=0, concat_axi...]
    dynamic_update_slice x16 -> x0, local copies, waits for them, and re-layouts: 22.2 us -> none  [local(): exposure = lax.map(tile_work, (tile_slots, geometry, absorption))]
    convert_element_type x9 -> x0, other arithmetic: 6.32 us -> none  [the longest x8 5.62 us: tile_work(): factor.astype(jnp.float32) * gathered.astype(jnp.float32)]
    dynamic_slice x24 -> x0, local copies, waits for them, and re-layouts: 5.99 us -> none  [the longest x8 5.83 us: local(): exposure = lax.map(tile_work, (tile_slots, geometry, absorption))]
    while x1 -> x0, local copies, waits for them, and re-layouts: 4.01 us -> none  [local(): lax.map(pick_rows, flat_list.reshape(-1, block_rows))]
  transfers between devices with their start and end apart: 3 -> 0, of which waited for: 2 -> 0; matrix products, arithmetic and copies ran while one was open for 10% -> 0% of each run, Pallas kernels for 0% -> 0%
where the time goes in v1:
time: 88.4 us; the launch traced here: 87.3 us
  Pallas kernels  81.4 us (92%)
  local copies, waits for them, and re-layouts  5.29 us (6%)
    pallas_call x1, Pallas kernels, local(): pl.pallas_call(kernel, out_shape=(jax.ShapeDtypeStruct((16, 128), F32), j...  81.4 us
    unnamed x3, local copies, waits for them, and re-layouts  5.29 us

profile of v1, /device:TPU:1, one launch (start us, length us, event | category | flops | bytes accessed | tf_op | source)
XLA Modules:
  0.0 87.3 jit_solution(10466921916649016161)
XLA Ops:
  0.6 81.4 %noise_map.1 = (f32[16,128]{1,0:T(8,128)}, f32[16,128]{1,0:T(8,128)}, f32[192,2048]{1,0:T(8,128)}) custom-call(bf16[192,512]{1,0:T(8,128)(2,1)} %bitcast.15, s32[64,128]{1,0:T(8,128)} %bitcast.16, s32[8,512]{1,0:T(8,128)} %slot_ref.1, bf16[8,256,512]{2,1,0:T(8,128)(2,1)} %geo_hbm.1, bf16[8,8,512]{2,1,0:T(8,128)(2,1)} %abs_ref.1, s32[24]{0:T(128)} %hour_ref.1, ...), custom_call_target="tpu_custom_call" | custom-call | tf_op jit(solution)/shard_map/noise_map/pallas_call | solution.py:258
  82.0 1.3 %copy.15 = f32[2048]{0:T(1024)} copy(f32[2048]{0:T(1024)} %bitcast.21) | data formatting | bytes 16384
  83.3 1.3 %copy.16 = f32[2048]{0:T(1024)} copy(f32[2048]{0:T(1024)} %bitcast.20) | data formatting | bytes 16384
  84.6 2.7 %copy.17 = f32[2048,192]{0,1:T(8,128)} copy(f32[2048,192]{0,1:T(8,128)} %bitcast.14) | data formatting | bytes 3145728

commit v2 on v1

--- a/solution.py
+++ b/solution.py
@@ -56,13 +56,12 @@
 
 
 def kernel(
-    em_ref, ps_ref, slot_ref, geo_hbm, abs_ref, hour_ref, dwell_ref, addr_ref, bld_ref,
-    level_ref, build_ref, expo_ref,
-    rows, outb, recv, rhs, acc, hi_ref, lo_ref, geo, weight, msg_out, msg_in,
-    geo_sem, self_sem, send_sem, recv_sem, msend_sem, mrecv_sem,
+    em_ref, ps_ref, slot_ref, geo_hbm, abs_ref, hour_ref, dwell_ref, addr_ref,
+    level_ref, msg_ref, expo_ref,
+    rows, outb, recv, rhs, acc, hi_ref, lo_ref, geo, weight, first, second, hots, out_a, in_a, out_b, in_b,
+    geo_sem, self_sem, send_sem, recv_sem, msend_sem, nsend_sem, mrecv_sem,
 ):
-    region, core = lax.axis_index("region"), lax.axis_index("band")
-    me = region * 2 + core
+    core = lax.axis_index("band")
     geo_copy = pltpu.make_async_copy(geo_hbm, geo, geo_sem)
     geo_copy.start()
     barrier = pltpu.get_barrier_semaphore()
@@ -141,6 +140,15 @@
         gain = jnp.where(r % HOURS == h, g.astype(F32), gain)
     weight[...] = scale * gain / HOURS
 
+    addr = permuted(
+        addr_ref[...], lambda k: pl.ds(k // 2 * 32 + k % 2, 16, stride=2), lambda k: pl.ds(k * 16, 16), first, second
+    )
+    addr_high = jnp.maximum(addr, 0) // 128
+    addr_low = jnp.where(addr >= 0, addr % 128, -1)
+    sub = lax.broadcasted_iota(I32, (128, 128), 0)
+    for c in range(CAP_ADDR):
+        hots[:, c * 128 : (c + 1) * 128] = jnp.where(sub == addr_low[c : c + 1], 1.0, 0.0).astype(BF16)
+
     acc[...] = jnp.zeros_like(acc)
     ROWS = 1024
 
@@ -205,36 +213,66 @@
 
     dwell = dwell_ref[...].astype(F32)
     table = jnp.concatenate([*split3(dwell * level_ref[...]), dwell.astype(BF16)], axis=0)
-    addr = addr_ref[...]
-    addr_high, addr_low = jnp.maximum(addr, 0) // 128, jnp.where(addr >= 0, addr % 128, -1)
-    sub = lax.broadcasted_iota(I32, (128, 128), 0)
+    found = jnp.dot(table, hots[...], preferred_element_type=F32)
+    level_rows = found[0:16] + found[16:32] + found[32:48]
     weighted, dwelt = [], []
     for c in range(CAP_ADDR):
-        hot = jnp.where(sub == addr_low[c : c + 1], 1.0, 0.0).astype(BF16)
-        found = jnp.dot(table, hot, preferred_element_type=F32)
-        level_rows = found[0:16] + found[16:32] + found[32:48]
+        lanes = slice(c * 128, (c + 1) * 128)
         mine = lax.broadcasted_iota(I32, (16, 128), 0) == addr_high[c : c + 1]
-        weighted.append(jnp.sum(jnp.where(mine, level_rows, 0.0), axis=0, keepdims=True))
-        dwelt.append(jnp.sum(jnp.where(mine, found[48:64], 0.0), axis=0, keepdims=True))
-    message = jnp.concatenate(weighted + dwelt + [jnp.zeros((96, 128), F32)], axis=0).T
-    msg_out[:, 0, :] = message
-    msg_in[pl.ds(me, 1)] = msg_out[pl.ds(me, 1)]
-
-    def post(step, carry):
-        to_region, to_core = peer(step)
+        weighted.append(jnp.sum(jnp.where(mine, level_rows[:, lanes], 0.0), axis=0, keepdims=True))
+        dwelt.append(jnp.sum(jnp.where(mine, found[48:64, lanes], 0.0), axis=0, keepdims=True))
+    out_a[...] = jnp.concatenate(weighted + dwelt + [jnp.zeros((96, 128), F32)], axis=0).T.reshape(8, 16, 128)
+    y, x, z, _ = my_place()
+    mine_a, mine_b = y * 2 + core, x * 4 + z
+    in_a[mine_a] = out_a[mine_a]
+    for k in range(1, 8):
+        to_y, to_core = (y + k // 2) % 4, (core + k % 2) % 2
         pltpu.make_async_remote_copy(
-            src_ref=msg_out.at[to_region * 2 + to_core], dst_ref=msg_in.at[me], send_sem=msend_sem, recv_sem=mrecv_sem,
-            device_id=(to_region, to_core), device_id_type=MESH,
+            src_ref=out_a.at[to_y * 2 + to_core], dst_ref=in_a.at[mine_a], send_sem=msend_sem, recv_sem=mrecv_sem.at[0],
+            device_id=(to_y * 16 + mine_b, to_core), device_id_type=MESH,
         ).start()
-        return carry
-
-    lax.fori_loop(1, DEVICES, post, 0)
-    all_in = msg_in.at[pl.ds(0, DEVICES - 1)]
-    pltpu.make_async_copy(all_in, all_in, mrecv_sem).wait()
-
-    got = msg_in[:, 0, :].T
-    bld = bld_ref[...]
+    seven = in_a.at[pl.ds(0, 7)]
+    pltpu.make_async_copy(seven, seven, mrecv_sem.at[0]).wait()
+    for k in range(8):
+        out_b[:, k, :] = in_a[k]
+    in_b[mine_b] = out_b[mine_b]
+    for k in range(1, 16):
+        to = ((x + k // 4) % 4) * 4 + (z + k % 4) % 4
+        pltpu.make_async_remote_copy(
+            src_ref=out_b.at[to], dst_ref=in_b.at[mine_b], send_sem=nsend_sem, recv_sem=mrecv_sem.at[1],
+            device_id=(y * 16 + to, core), device_id_type=MESH,
+        ).start()
+    fifteen = in_b.at[pl.ds(0, 15)]
+    pltpu.make_async_copy(fifteen, fifteen, mrecv_sem.at[1]).wait()
+    msg_ref[...] = in_b[...]
+
+    all_out = outb.at[pl.ds(0, DEVICES - 1)]
+    pltpu.make_async_copy(all_out, all_out, send_sem).wait()
+    sent_a, sent_b = out_a.at[pl.ds(0, 7)], out_b.at[pl.ds(0, 15)]
+    pltpu.make_async_copy(sent_a, sent_a, msend_sem).wait()
+    pltpu.make_async_copy(sent_b, sent_b, nsend_sem).wait()
+
+
+def permuted(values, in_rows, out_rows, first, second):
+    first[...] = jnp.concatenate([values.astype(F32), jnp.zeros((112, 128), F32)], axis=0).T
+    for k in range(8):
+        second[out_rows(k), :] = first[in_rows(k), :]
+    return second[...].T[0:16].astype(I32)
+
+
+def finish(level_in, msg_in, bld_ref, expo_in, level_ref, build_ref, expo_ref, first, second, sems):
+    pieces = []
+    for k in range(4):
+        cut = pl.ds(k * (WIDTH // 4), WIDTH // 4)
+        pieces.append(pltpu.make_async_copy(expo_in.at[cut], expo_ref.at[cut], sems.at[k]))
+        pieces[k].start()
+    level_ref[...] = level_in[...]
+    got = msg_in[...].reshape(128, 128).T
+    bld = permuted(
+        bld_ref[...], lambda k: pl.ds(k // 2 * 32 + k % 2, 16, stride=2), lambda k: pl.ds(k, 16, stride=8), first, second
+    )
     bld_high, bld_low = bld // 128, bld % 128
+    sub = lax.broadcasted_iota(I32, (128, 128), 0)
     lhs, hots = [], []
     for c in range(CAP_ADDR):
         mine = lax.broadcasted_iota(I32, (16, 128), 0) == bld_high[c : c + 1]
@@ -246,23 +284,20 @@
         jnp.concatenate(lhs, axis=1), jnp.concatenate(hots, axis=1), (((1,), (1,)), ((), ())), preferred_element_type=F32
     )
     build_ref[...] = (sums[0:16] + sums[16:32] + sums[32:48]) / jnp.maximum(sums[48:64], 1.0)
-
-    all_out = outb.at[pl.ds(0, DEVICES - 1)]
-    pltpu.make_async_copy(all_out, all_out, send_sem).wait()
-    all_mail = msg_out.at[pl.ds(0, DEVICES - 1)]
-    pltpu.make_async_copy(all_mail, all_mail, msend_sem).wait()
+    for piece in pieces:
+        piece.wait()
 
 
 def local(emission, path_sends, tile_slots, geometry, absorption, hour_period, dwellings, addr_sends, addr_building):
     vmem = pl.BlockSpec(memory_space=pltpu.VMEM)
-    level, building, exposure = pl.pallas_call(
+    level, messages, exposure = pl.pallas_call(
         kernel,
         out_shape=(
             jax.ShapeDtypeStruct((16, 128), F32),
-            jax.ShapeDtypeStruct((16, 128), F32),
+            jax.ShapeDtypeStruct((16, 8, 128), F32),
             jax.ShapeDtypeStruct((WIDTH, TILE_DEV * RECV_TILE), F32),
         ),
-        in_specs=[vmem, vmem, vmem, pl.BlockSpec(memory_space=pl.ANY), vmem, pl.BlockSpec(memory_space=pltpu.SMEM), vmem, vmem, vmem],
+        in_specs=[vmem, vmem, vmem, pl.BlockSpec(memory_space=pl.ANY), vmem, pl.BlockSpec(memory_space=pltpu.SMEM), vmem, vmem],
         out_specs=(vmem, vmem, vmem),
         scratch_shapes=[
             pltpu.VMEM((SEG_DEV, 256), BF16),
@@ -274,14 +309,20 @@
             pltpu.VMEM((PATHS, 128), BF16),
             pltpu.VMEM((TILE_DEV, RECV_TILE, PATHS_TILE), BF16),
             pltpu.VMEM((WIDTH, 128), F32),
-            pltpu.VMEM((DEVICES, 1, 128), F32),
-            pltpu.VMEM((DEVICES, 1, 128), F32),
+            pltpu.VMEM((128, 128), F32),
+            pltpu.VMEM((128, 128), F32),
+            pltpu.VMEM((128, 2048), BF16),
+            pltpu.VMEM((8, 16, 128), F32),
+            pltpu.VMEM((8, 16, 128), F32),
+            pltpu.VMEM((16, 8, 128), F32),
+            pltpu.VMEM((16, 8, 128), F32),
             pltpu.SemaphoreType.DMA,
             pltpu.SemaphoreType.DMA,
             pltpu.SemaphoreType.DMA,
             pltpu.SemaphoreType.DMA((DEVICES // GROUP,)),
             pltpu.SemaphoreType.DMA,
             pltpu.SemaphoreType.DMA,
+            pltpu.SemaphoreType.DMA((2,)),
         ],
         compiler_params=pltpu.CompilerParams(collective_id=0, has_side_effects=True, vmem_limit_bytes=56 * 2**20),
         name="noise_map",
@@ -294,8 +335,21 @@
         hour_period,
         dwellings.reshape(16, 128),
         addr_sends[0].T,
-        addr_building[0].T,
     )
+    hbm = pl.BlockSpec(memory_space=pl.ANY)
+    level, building, exposure = pl.pallas_call(
+        finish,
+        out_shape=(
+            jax.ShapeDtypeStruct((16, 128), F32),
+            jax.ShapeDtypeStruct((16, 128), F32),
+            jax.ShapeDtypeStruct((WIDTH, TILE_DEV * RECV_TILE), F32),
+        ),
+        in_specs=[vmem, vmem, vmem, hbm],
+        out_specs=(vmem, vmem, hbm),
+        scratch_shapes=[pltpu.VMEM((128, 128), F32), pltpu.VMEM((128, 128), F32), pltpu.SemaphoreType.DMA((4,))],
+        compiler_params=pltpu.CompilerParams(vmem_limit_bytes=16 * 2**20),
+        name="buildings",
+    )(level, messages, addr_building[0].T, exposure)
     return level.reshape(-1), building.reshape(-1), exposure.T
 
 

time: 88.4 us -> 81.7 us (0.924)
  Pallas kernels: 81.4 us -> 77.9 us
  local copies, waits for them, and re-layouts: 5.29 us -> 2.94 us
    pallas_call x1, Pallas kernels: 81.4 us -> 76.1 us  [local(): pl.pallas_call(kernel, out_shape=(jax.ShapeDtypeStruct((16, 128), F32), j...]
    unnamed x3 -> x8, local copies, waits for them, and re-layouts: 5.29 us -> 2.94 us
    pallas_call x0 -> x1, Pallas kernels: none -> 1.77 us  [local(): pl.pallas_call(finish, out_shape=(jax.ShapeDtypeStruct((16, 128), F32), j...]
where the time goes in v2:
time: 81.7 us; the launch traced here: 81.5 us
  Pallas kernels  77.9 us (95%)
  local copies, waits for them, and re-layouts  2.94 us (4%)
    pallas_call x1, Pallas kernels, local(): pl.pallas_call(kernel, out_shape=(jax.ShapeDtypeStruct((16, 128), F32), j...  76.1 us
    unnamed x8, local copies, waits for them, and re-layouts  2.94 us
    pallas_call x1, Pallas kernels, local(): pl.pallas_call(finish, out_shape=(jax.ShapeDtypeStruct((16, 128), F32), j...  1.77 us

profile of v2, /device:TPU:1, one launch (start us, length us, event | category | flops | bytes accessed | tf_op | source)
XLA Modules:
  0.0 81.5 jit_solution(16213179065034435501)
XLA Ops:
  0.6 0.0 copy-start.2
  0.6 76.1 %noise_map.1 = (f32[16,128]{1,0:T(8,128)}, f32[16,8,128]{2,1,0:T(8,128)}, f32[192,2048]{1,0:T(8,128)}) custom-call(bf16[192,512]{1,0:T(8,128)(2,1)} %bitcast.15, s32[64,128]{1,0:T(8,128)} %bitcast.16, s32[8,512]{1,0:T(8,128)} %slot_ref.1, bf16[8,256,512]{2,1,0:T(8,128)(2,1)} %geo_hbm.1, bf16[8,8,512]{2,1,0:T(8,128)(2,1)} %abs_ref.1, s32[24]{0:T(128)} %hour_ref.1, ...), custom_call_target="tpu_custom_call" | custom-call | tf_op jit(solution)/shard_map/noise_map/pallas_call | solution.py:293
  76.7 0.0 copy-done.2
  76.8 0.0 copy-start
  76.8 1.4 %copy-done = f32[192,2048]{1,0:T(8,128)S(1)} copy-done((f32[192,2048]{1,0:T(8,128)S(1)}, f32[192,2048]{1,0:T(8,128)}, u32[]{:S(2)}) %copy-start) | copy-done | bytes 1572888
  78.2 0.0 copy-start.1
  78.2 0.8 %copy-done.1 = f32[16,8,128]{2,1,0:T(8,128)S(1)} copy-done((f32[16,8,128]{2,1,0:T(8,128)S(1)}, f32[16,8,128]{2,1,0:T(8,128)}, u32[]{:S(2)}) %copy-start.1) | copy-done | bytes 65560
  79.0 0.0 copy-start.3
  79.0 0.7 copy-done.3
  79.7 1.8 %buildings.1 = (f32[16,128]{1,0:T(8,128)}, f32[16,128]{1,0:T(8,128)}, f32[192,2048]{1,0:T(8,128)}) custom-call(f32[16,128]{1,0:T(8,128)S(1)} %copy-done.3, f32[16,8,128]{2,1,0:T(8,128)S(1)} %copy-done.1, s32[16,128]{1,0:T(8,128)S(1)} %bitcast.14, f32[192,2048]{1,0:T(8,128)S(1)} %copy-done), custom_call_target="tpu_custom_call" | custom-call | tf_op jit(solution)/shard_map/buildings/pallas_call | solution.py:340
Async XLA Ops:
  0.6 76.1 %copy-start.2 = (s32[1,128,16]{1,2,0:T(8,128)S(1)}, s32[1,128,16]{1,2,0:T(8,128)}, u32[]{:S(2)}) copy-start(s32[1,128,16]{1,2,0:T(8,128)} %param.17) | copy-start | bytes 24580
  76.8 1.4 %copy-start = (f32[192,2048]{1,0:T(8,128)S(1)}, f32[192,2048]{1,0:T(8,128)}, u32[]{:S(2)}) copy-start(f32[192,2048]{1,0:T(8,128)} %get-tuple-element.11.expo_in) | copy-start | bytes 4718596
  78.2 0.8 %copy-start.1 = (f32[16,8,128]{2,1,0:T(8,128)S(1)}, f32[16,8,128]{2,1,0:T(8,128)}, u32[]{:S(2)}) copy-start(f32[16,8,128]{2,1,0:T(8,128)} %get-tuple-element.10.msg_in) | copy-start | bytes 196612
  79.0 0.7 copy-start.3

commit v3 on v2

v3 whole, which is shorter than its diff:
```python
import math

import jax
import jax.numpy as jnp
from jax import lax
from jax.experimental import pallas as pl
from jax.experimental.pallas import tpu as pltpu
from jax.sharding import PartitionSpec as P

BANDS = 8
HOURS = 24
WIDTH = BANDS * HOURS
SEG_DEV = 512
CAP = 64
TILE_DEV = 8
RECV_TILE = 256
PATHS_TILE = 512
CAP_ADDR = 16
DEVICES = 128
PATHS = TILE_DEV * PATHS_TILE
PART = 64
STRIDE = (16, 4, 1)
PLANE = ((1, 2), (0, 2), (0, 1))
SPAN = 4096
LAG = 2
A_WEIGHTING_DB = (-26.2, -16.1, -8.6, -3.2, 0.0, 1.2, 1.0, -1.1)
MESH = pl.DeviceIdType.MESH
BF16, F32, I32 = jnp.bfloat16, jnp.float32, jnp.int32


def split3(value):
    high = value.astype(BF16)
    rest = value - high.astype(F32)
    mid = rest.astype(BF16)
    return high, mid, (rest - mid.astype(F32)).astype(BF16)


def my_place():
    region, core = lax.axis_index("region"), lax.axis_index("band")
    return (region // 16, (region // 4) % 4, region % 4), core


def one_hot(row, count):
    lines = lax.broadcasted_iota(I32, (count, row.shape[1]), 0)
    return jnp.where(lines == row, 1.0, 0.0).astype(BF16)


def drain(ref, sem):
    pltpu.make_async_copy(ref, ref, sem).wait()


def kernel(
    em_ref, ps_ref, slot_ref, geo_hbm, abs_ref, hour_ref, dwell_ref, addr_ref,
    level_ref, msg_ref, expo_ref,
    even, odd, lines, lists, outb, recv, acc, label, quarter, geo, weight, first, second, hots, out_a, in_a, out_b, in_b,
    geo_sem, line_sem, list_sem, send_sem, line_in, list_in, recv_sem, msend_sem, nsend_sem, mrecv_sem,
):
    at, core = my_place()
    y, x, z = at
    geo_copy = pltpu.make_async_copy(geo_hbm, geo, geo_sem)
    geo_copy.start()
    barrier = pltpu.get_barrier_semaphore()
    peers = 0
    for dy in range(4):
        for dx in range(4):
            for dz in range(4):
                for dc in range(2):
                    if 0 in (dy, dx, dz) and (dy, dx, dz, dc) != (0, 0, 0, 0):
                        to = ((y + dy) % 4) * 16 + ((x + dx) % 4) * 4 + (z + dz) % 4
                        pl.semaphore_signal(barrier, inc=1, device_id=(to, (core + dc) % 2), device_id_type=MESH)
                        peers += 1

    entries = ps_ref[...].astype(F32)
    first[...] = jnp.concatenate([entries, entries], axis=0).T
    zero, one = first[pl.ds(0, 64, stride=2), :], first[pl.ds(1, 64, stride=2), :]
    left = lax.broadcasted_iota(I32, (64, 128), 1) < 64
    both, swapped = jnp.where(left, zero, one), jnp.where(left, one, zero)
    for a in range(4):
        for b in range(4):
            cut = slice((a * 4 + b) * 4, (a * 4 + b) * 4 + 4)
            even[a, b, :, 0, :] = both[cut]
            odd[a, b, :, 0, :] = swapped[cut]

    pl.semaphore_wait(barrier, peers)

    def plane_of(ref, p, where):
        return ref.at[where] if p == 0 else ref.at[:, where] if p == 1 else ref.at[:, :, where]

    for j in (1, 3, 2):
        for p in range(3):
            where = (at[p] + j) % 4
            to = sum(STRIDE[q] * (where if q == p else at[q]) for q in range(3))
            pltpu.make_async_remote_copy(
                src_ref=plane_of(odd if j % 2 else even, p, where), dst_ref=lists.at[p * 4 + j],
                send_sem=list_sem, recv_sem=list_in.at[p], device_id=(to, core), device_id_type=MESH,
            ).start()
            pltpu.make_async_remote_copy(
                src_ref=em_ref.at[pl.ds(p * PART, PART)], dst_ref=lines.at[p * 4 + j],
                send_sem=line_sem, recv_sem=line_in.at[p], device_id=(to, core), device_id_type=MESH,
            ).start()
    for p in range(3):
        lines[p * 4] = em_ref[p * PART : (p + 1) * PART, :]
        lists[p * 4] = plane_of(even, p, at[p])[...]

    def pick(u, carry):
        for p in range(3):
            b1, b2 = PLANE[p]
            line1 = (at[b1] + u) % 4
            line2 = [(at[b2] + v) % 4 for v in range(4)]

            @pl.when(u == 0)
            def _():
                drain(lists.at[pl.ds(p * 4 + 1, 3)], list_in.at[p])
                drain(lines.at[pl.ds(p * 4 + 1, 3)], line_in.at[p])

            found = []
            for i in range(4):
                row = jnp.concatenate([lists[p * 4 + i, line1, v] for v in line2], axis=1)
                upper = row >= 256.0
                table = one_hot(jnp.where(upper, row - 256.0, row).astype(I32), 256)
                source = lines[p * 4 + i]
                halves = jnp.concatenate([source[:, 0:256], source[:, 256:512]], axis=0)
                out = jnp.dot(halves, table, preferred_element_type=F32)
                found.append(jnp.where(upper, out[PART:], out[:PART]))
            low = lax.broadcasted_iota(I32, (PART, 512), 1) % 128 < 64
            for k in range(2):
                pairs = []
                for i in (0, 2):
                    a, b = (found[i], found[i + 1]) if k == 0 else (found[i + 1], found[i])
                    pairs.append(jnp.where(low, a, b).astype(BF16))
                for v in range(4):
                    cut = slice(v * 128, (v + 1) * 128)
                    outb[(p * 4 + u) * 8 + k * 4 + v] = jnp.concatenate([pairs[0][:, cut], pairs[1][:, cut]], axis=1)
            for dc in range(2):
                to_core = (core + dc) % 2
                for v in range(4):
                    to = STRIDE[p] * at[p] + STRIDE[b1] * line1 + STRIDE[b2] * line2[v]
                    copy = pltpu.make_async_remote_copy(
                        src_ref=outb.at[(p * 4 + u) * 8 + to_core * 4 + v], dst_ref=recv.at[(p * 4 + u) * 8 + dc * 4 + v],
                        send_sem=send_sem, recv_sem=recv_sem.at[p * 4 + u], device_id=(to, to_core), device_id_type=MESH,
                    )
                    if dc or v:
                        copy.start()
                    else:

                        @pl.when(u > 0)
                        def _():
                            copy.start()

                        @pl.when(u == 0)
                        def _():
                            recv[p * 32] = outb[p * 32 + core * 4]

        return carry

    slots = slot_ref[...]
    safe = jnp.maximum(slots, 0)
    source, entry = safe // CAP, safe % CAP
    apart = (
        (y + 4 - source // 32) % 4, (x + 4 - (source // 8) % 4) % 4, (z + 4 - (source // 2) % 4) % 4,
    )
    other = (core + 2 - source % 2) % 2
    for p in range(3):
        b1, b2 = PLANE[p]
        lane = (apart[p] // 2) * 128 + ((apart[p] + core) % 2) * 64 + entry
        group = jnp.where(slots >= 0, apart[b1] * 2 + other, -1)
        for g in range(8):
            label[p * 8 + g] = jnp.where(group == g, lane, -1)
        quarter[p] = apart[b2]

    r = lax.broadcasted_iota(I32, (WIDTH, 128), 0)
    scale = jnp.zeros((WIDTH, 128), F32)
    for b in range(BANDS):
        scale = jnp.where(r // HOURS == b, jnp.float32(10.0 ** (A_WEIGHTING_DB[b] / 10.0)), scale)
    gain = jnp.zeros((WIDTH, 128), F32)
    for h in range(HOURS):
        period = hour_ref[h]
        g = jnp.where(period == 0, 1.0, jnp.where(period == 1, jnp.float32(10.0**0.5), jnp.where(period == 2, 10.0, 0.0)))
        gain = jnp.where(r % HOURS == h, g.astype(F32), gain)
    weight[...] = scale * gain / HOURS

    addr = permuted(
        addr_ref[...], lambda k: pl.ds(k // 2 * 32 + k % 2, 16, stride=2), lambda k: pl.ds(k * 16, 16), first, second
    )
    addr_high = jnp.maximum(addr, 0) // 128
    addr_low = jnp.where(addr >= 0, addr % 128, -1)
    for c in range(CAP_ADDR):
        hots[:, c * 128 : (c + 1) * 128] = one_hot(addr_low[c : c + 1], 128)
    acc[...] = jnp.zeros_like(acc)

    def gather(u, carry):
        for p in range(3):
            step = p * 4 + u

            @pl.when(u == 0)
            def _():
                drain(recv.at[pl.ds(p * 32 + 1, 7)], recv_sem.at[step])

            @pl.when(u > 0)
            def _():
                drain(recv.at[pl.ds(step * 8, 8)], recv_sem.at[step])

            def some_paths(n, inner):
                def row_of(ref, index):
                    first_tile = n * (SPAN // PATHS_TILE)
                    return jnp.concatenate([ref[index, pl.ds(first_tile + m, 1), :] for m in range(SPAN // PATHS_TILE)], axis=1)

                table = jnp.concatenate([one_hot(row_of(label, p * 8 + u * 2 + dc), 256) for dc in range(2)], axis=0)
                data = jnp.concatenate(
                    [recv[pl.ds(step * 8 + dc * 4, 4)].reshape(4 * PART, 256) for dc in range(2)], axis=1
                )
                out = jnp.dot(data, table, preferred_element_type=F32)
                which = row_of(quarter, p)
                out = [out[v * PART : (v + 1) * PART] for v in range(4)]
                mine = jnp.where(which < 2, jnp.where(which == 0, out[0], out[1]), jnp.where(which == 2, out[2], out[3]))
                cut = (slice(p * PART, (p + 1) * PART), pl.ds(pl.multiple_of(n * SPAN, SPAN), SPAN))
                acc[cut] = acc[cut] + mine
                return inner

            lax.fori_loop(0, PATHS // SPAN, some_paths, 0)
        return carry

    def turn(u, carry):
        @pl.when(u < 4)
        def _():
            pick(u, 0)

        @pl.when(u >= LAG)
        def _():
            gather(u - LAG, 0)

        return carry

    lax.fori_loop(0, 4 + LAG, turn, 0)
    geo_copy.wait()

    def tile(t, carry):
        gathered = acc[:, pl.ds(pl.multiple_of(t * PATHS_TILE, PATHS_TILE), PATHS_TILE)]
        damp = abs_ref[t].astype(F32)
        factor = jnp.concatenate(
            [jnp.broadcast_to(damp[b : b + 1], (HOURS, PATHS_TILE)) for b in range(BANDS)], axis=0
        )
        mixed = (factor * gathered).astype(BF16)
        exposure = lax.dot_general(mixed, geo[t], (((1,), (1,)), ((), ())), preferred_element_type=F32)
        expo_ref[:, pl.ds(pl.multiple_of(t * RECV_TILE, RECV_TILE), RECV_TILE)] = exposure
        for half in range(2):
            energy = jnp.sum(exposure[:, half * 128 : (half + 1) * 128] * weight[...], axis=0, keepdims=True)
            level_ref[pl.ds(2 * t + half, 1), :] = jnp.log(energy) * jnp.float32(1.0 / math.log(10.0))
        return carry

    lax.fori_loop(0, TILE_DEV, tile, 0)

    dwell = dwell_ref[...].astype(F32)
    table = jnp.concatenate([*split3(dwell * level_ref[...]), dwell.astype(BF16)], axis=0)
    found = jnp.dot(table, hots[...], preferred_element_type=F32)
    level_rows = found[0:16] + found[16:32] + found[32:48]
    weighted, dwelt = [], []
    for c in range(CAP_ADDR):
        lanes = slice(c * 128, (c + 1) * 128)
        mine = lax.broadcasted_iota(I32, (16, 128), 0) == addr_high[c : c + 1]
        weighted.append(jnp.sum(jnp.where(mine, level_rows[:, lanes], 0.0), axis=0, keepdims=True))
        dwelt.append(jnp.sum(jnp.where(mine, found[48:64, lanes], 0.0), axis=0, keepdims=True))
    out_a[...] = jnp.concatenate(weighted + dwelt + [jnp.zeros((96, 128), F32)], axis=0).T.reshape(8, 16, 128)
    mine_a, mine_b = y * 2 + core, x * 4 + z
    in_a[mine_a] = out_a[mine_a]
    for k in range(1, 8):
        to_y, to_core = (y + k // 2) % 4, (core + k % 2) % 2
        pltpu.make_async_remote_copy(
            src_ref=out_a.at[to_y * 2 + to_core], dst_ref=in_a.at[mine_a], send_sem=msend_sem, recv_sem=mrecv_sem.at[0],
            device_id=(to_y * 16 + mine_b, to_core), device_id_type=MESH,
        ).start()
    seven = in_a.at[pl.ds(0, 7)]
    pltpu.make_async_copy(seven, seven, mrecv_sem.at[0]).wait()
    for k in range(8):
        out_b[:, k, :] = in_a[k]
    in_b[mine_b] = out_b[mine_b]
    for k in range(1, 16):
        to = ((x + k // 4) % 4) * 4 + (z + k % 4) % 4
        pltpu.make_async_remote_copy(
            src_ref=out_b.at[to], dst_ref=in_b.at[mine_b], send_sem=nsend_sem, recv_sem=mrecv_sem.at[1],
            device_id=(y * 16 + to, core), device_id_type=MESH,
        ).start()
    fifteen = in_b.at[pl.ds(0, 15)]
    pltpu.make_async_copy(fifteen, fifteen, mrecv_sem.at[1]).wait()
    msg_ref[...] = in_b[...]

    drain(lists.at[pl.ds(0, 9)], list_sem)
    drain(lines.at[pl.ds(0, 9)], line_sem)
    drain(outb.at[pl.ds(0, 93)], send_sem)
    drain(out_a.at[pl.ds(0, 7)], msend_sem)
    drain(out_b.at[pl.ds(0, 15)], nsend_sem)


def permuted(values, in_rows, out_rows, first, second):
    first[...] = jnp.concatenate([values.astype(F32), jnp.zeros((112, 128), F32)], axis=0).T
    for k in range(8):
        second[out_rows(k), :] = first[in_rows(k), :]
    return second[...].T[0:16].astype(I32)


def finish(level_in, msg_in, bld_ref, expo_in, level_ref, build_ref, expo_ref, first, second, sems):
    pieces = []
    for k in range(4):
        cut = pl.ds(k * (WIDTH // 4), WIDTH // 4)
        pieces.append(pltpu.make_async_copy(expo_in.at[cut], expo_ref.at[cut], sems.at[k]))
        pieces[k].start()
    level_ref[...] = level_in[...]
    got = msg_in[...].reshape(128, 128).T
    bld = permuted(
        bld_ref[...], lambda k: pl.ds(k // 2 * 32 + k % 2, 16, stride=2), lambda k: pl.ds(k, 16, stride=8), first, second
    )
    bld_high, bld_low = bld // 128, bld % 128
    sub = lax.broadcasted_iota(I32, (128, 128), 0)
    lhs, hots = [], []
    for c in range(CAP_ADDR):
        mine = lax.broadcasted_iota(I32, (16, 128), 0) == bld_high[c : c + 1]
        spread = jnp.where(mine, got[c : c + 1], 0.0)
        count = jnp.where(mine, got[16 + c : 17 + c], 0.0)
        lhs.append(jnp.concatenate([*split3(spread), count.astype(BF16)], axis=0))
        hots.append(jnp.where(sub == bld_low[c : c + 1], 1.0, 0.0).astype(BF16))
    sums = lax.dot_general(
        jnp.concatenate(lhs, axis=1), jnp.concatenate(hots, axis=1), (((1,), (1,)), ((), ())), preferred_element_type=F32
    )
    build_ref[...] = (sums[0:16] + sums[16:32] + sums[32:48]) / jnp.maximum(sums[48:64], 1.0)
    for piece in pieces:
        piece.wait()


def local(emission, path_sends, tile_slots, geometry, absorption, hour_period, dwellings, addr_sends, addr_building):
    vmem = pl.BlockSpec(memory_space=pltpu.VMEM)
    level, messages, exposure = pl.pallas_call(
        kernel,
        out_shape=(
            jax.ShapeDtypeStruct((16, 128), F32),
            jax.ShapeDtypeStruct((16, 8, 128), F32),
            jax.ShapeDtypeStruct((WIDTH, TILE_DEV * RECV_TILE), F32),
        ),
        in_specs=[vmem, vmem, vmem, pl.BlockSpec(memory_space=pl.ANY), vmem, pl.BlockSpec(memory_space=pltpu.SMEM), vmem, vmem],
        out_specs=(vmem, vmem, vmem),
        scratch_shapes=[
            pltpu.VMEM((4, 4, 4, 1, 128), F32),
            pltpu.VMEM((4, 4, 4, 1, 128), F32),
            pltpu.VMEM((12, PART, SEG_DEV), BF16),
            pltpu.VMEM((12, 4, 4, 1, 128), F32),
            pltpu.VMEM((96, PART, 256), BF16),
            pltpu.VMEM((96, PART, 256), BF16),
            pltpu.VMEM((WIDTH, PATHS), F32),
            pltpu.VMEM((24, TILE_DEV, PATHS_TILE), I32),
            pltpu.VMEM((3, TILE_DEV, PATHS_TILE), I32),
            pltpu.VMEM((TILE_DEV, RECV_TILE, PATHS_TILE), BF16),
            pltpu.VMEM((WIDTH, 128), F32),
            pltpu.VMEM((128, 128), F32),
            pltpu.VMEM((128, 128), F32),
            pltpu.VMEM((128, 2048), BF16),
            pltpu.VMEM((8, 16, 128), F32),
            pltpu.VMEM((8, 16, 128), F32),
            pltpu.VMEM((16, 8, 128), F32),
            pltpu.VMEM((16, 8, 128), F32),
            pltpu.SemaphoreType.DMA,
            pltpu.SemaphoreType.DMA,
            pltpu.SemaphoreType.DMA,
            pltpu.SemaphoreType.DMA,
            pltpu.SemaphoreType.DMA((3,)),
            pltpu.SemaphoreType.DMA((3,)),
            pltpu.SemaphoreType.DMA((12,)),
            pltpu.SemaphoreType.DMA,
            pltpu.SemaphoreType.DMA,
            pltpu.SemaphoreType.DMA((2,)),
        ],
        compiler_params=pltpu.CompilerParams(collective_id=0, has_side_effects=True, vmem_limit_bytes=56 * 2**20),
        name="noise_map",
    )(
        emission.T,
        path_sends[0].T,
        tile_slots,
        geometry,
        absorption,
        hour_period,
        dwellings.reshape(16, 128),
        addr_sends[0].T,
    )
    hbm = pl.BlockSpec(memory_space=pl.ANY)
    level, building, exposure = pl.pallas_call(
        finish,
        out_shape=(
            jax.ShapeDtypeStruct((16, 128), F32),
            jax.ShapeDtypeStruct((16, 128), F32),
            jax.ShapeDtypeStruct((WIDTH, TILE_DEV * RECV_TILE), F32),
        ),
        in_specs=[vmem, vmem, vmem, hbm],
        out_specs=(vmem, vmem, hbm),
        scratch_shapes=[pltpu.VMEM((128, 128), F32), pltpu.VMEM((128, 128), F32), pltpu.SemaphoreType.DMA((4,))],
        compiler_params=pltpu.CompilerParams(vmem_limit_bytes=16 * 2**20),
        name="buildings",
    )(level, messages, addr_building[0].T, exposure)
    return level.reshape(-1), building.reshape(-1), exposure.T


def solution(mesh):
    both = ("region", "band")
    in_specs = (P(both, None), P(both, None, None), P(both, None), P(both, None, None), P(both, None, None), P(), P(both), P(both, None, None), P(both, None, None))
    out_specs = (P(both), P(both), P(both, None))
    return jax.shard_map(local, mesh=mesh, in_specs=in_specs, out_specs=out_specs, check_vma=False)
```

time: 81.7 us -> 71.2 us (0.87)
  Pallas kernels: 77.9 us -> 67.3 us
    pallas_call x1, Pallas kernels: 76.1 us -> 65.5 us  [local(): pl.pallas_call(kernel, out_shape=(jax.ShapeDtypeStruct((16, 128), F32), j...]
where the time goes in v3:
time: 71.2 us; the launch traced here: 70.9 us
  Pallas kernels  67.3 us (95%)
  local copies, waits for them, and re-layouts  2.94 us (4%)
    pallas_call x1, Pallas kernels, local(): pl.pallas_call(kernel, out_shape=(jax.ShapeDtypeStruct((16, 128), F32), j...  65.5 us
    unnamed x8, local copies, waits for them, and re-layouts  2.94 us
    pallas_call x1, Pallas kernels, local(): pl.pallas_call(finish, out_shape=(jax.ShapeDtypeStruct((16, 128), F32), j...  1.77 us

profile of v3, /device:TPU:1, one launch (start us, length us, event | category | flops | bytes accessed | tf_op | source)
XLA Modules:
  0.0 70.9 jit_solution(2681881333599971327)
XLA Ops:
  0.6 0.0 copy-start.2
  0.6 65.5 %noise_map.1 = (f32[16,128]{1,0:T(8,128)}, f32[16,8,128]{2,1,0:T(8,128)}, f32[192,2048]{1,0:T(8,128)}) custom-call(bf16[192,512]{1,0:T(8,128)(2,1)} %bitcast.15, s32[64,128]{1,0:T(8,128)} %bitcast.16, s32[8,512]{1,0:T(8,128)} %slot_ref.1, bf16[8,256,512]{2,1,0:T(8,128)(2,1)} %geo_hbm.1, bf16[8,8,512]{2,1,0:T(8,128)(2,1)} %abs_ref.1, s32[24]{0:T(128)} %hour_ref.1, ...), custom_call_target="tpu_custom_call" | custom-call | tf_op jit(solution)/shard_map/noise_map/pallas_call | solution.py:331
  66.2 0.0 copy-done.2
  66.2 0.0 copy-start
  66.2 1.4 %copy-done = f32[192,2048]{1,0:T(8,128)S(1)} copy-done((f32[192,2048]{1,0:T(8,128)S(1)}, f32[192,2048]{1,0:T(8,128)}, u32[]{:S(2)}) %copy-start) | copy-done | bytes 1572888
  67.6 0.0 copy-start.1
  67.6 0.8 %copy-done.1 = f32[16,8,128]{2,1,0:T(8,128)S(1)} copy-done((f32[16,8,128]{2,1,0:T(8,128)S(1)}, f32[16,8,128]{2,1,0:T(8,128)}, u32[]{:S(2)}) %copy-start.1) | copy-done | bytes 65560
  68.5 0.0 copy-start.3
  68.5 0.7 copy-done.3
  69.2 1.8 %buildings.1 = (f32[16,128]{1,0:T(8,128)}, f32[16,128]{1,0:T(8,128)}, f32[192,2048]{1,0:T(8,128)}) custom-call(f32[16,128]{1,0:T(8,128)S(1)} %copy-done.3, f32[16,8,128]{2,1,0:T(8,128)S(1)} %copy-done.1, s32[16,128]{1,0:T(8,128)S(1)} %bitcast.14, f32[192,2048]{1,0:T(8,128)S(1)} %copy-done), custom_call_target="tpu_custom_call" | custom-call | tf_op jit(solution)/shard_map/buildings/pallas_call | solution.py:383
Async XLA Ops:
  0.6 65.6 %copy-start.2 = (s32[1,128,16]{1,2,0:T(8,128)S(1)}, s32[1,128,16]{1,2,0:T(8,128)}, u32[]{:S(2)}) copy-start(s32[1,128,16]{1,2,0:T(8,128)} %param.17) | copy-start | bytes 24580
  66.2 1.4 %copy-start = (f32[192,2048]{1,0:T(8,128)S(1)}, f32[192,2048]{1,0:T(8,128)}, u32[]{:S(2)}) copy-start(f32[192,2048]{1,0:T(8,128)} %get-tuple-element.11.expo_in) | copy-start | bytes 4718596
  67.6 0.8 %copy-start.1 = (f32[16,8,128]{2,1,0:T(8,128)S(1)}, f32[16,8,128]{2,1,0:T(8,128)}, u32[]{:S(2)}) copy-start(f32[16,8,128]{2,1,0:T(8,128)} %get-tuple-element.10.msg_in) | copy-start | bytes 196612
  68.5 0.7 copy-start.3

commit v4 on v3

v4 whole, which is shorter than its diff:
```python
import math

import jax
import jax.numpy as jnp
from jax import lax
from jax.experimental import pallas as pl
from jax.experimental.pallas import tpu as pltpu
from jax.sharding import PartitionSpec as P

BANDS = 8
HOURS = 24
WIDTH = BANDS * HOURS
SEG_DEV = 512
CAP = 64
TILE_DEV = 8
RECV_TILE = 256
PATHS_TILE = 512
CAP_ADDR = 16
DEVICES = 128
PATHS = TILE_DEV * PATHS_TILE
PART = 64
STRIDE = (16, 4, 1)
PLANE = ((1, 2), (0, 2), (0, 1))
SPAN = 4096
CUTS = 6
AHEAD = 7
A_WEIGHTING_DB = (-26.2, -16.1, -8.6, -3.2, 0.0, 1.2, 1.0, -1.1)
MESH = pl.DeviceIdType.MESH
BF16, F32, I32 = jnp.bfloat16, jnp.float32, jnp.int32


def split3(value):
    high = value.astype(BF16)
    rest = value - high.astype(F32)
    mid = rest.astype(BF16)
    return high, mid, (rest - mid.astype(F32)).astype(BF16)


def my_place():
    region, core = lax.axis_index("region"), lax.axis_index("band")
    return (region // 16, (region // 4) % 4, region % 4), core


def one_hot(row, count):
    lines = lax.broadcasted_iota(I32, (count, row.shape[1]), 0)
    return jnp.where(lines == row, 1.0, 0.0).astype(BF16)


def drain(ref, sem):
    pltpu.make_async_copy(ref, ref, sem).wait()


def kernel(
    em_hbm, ps_hbm, slot_hbm, geo_hbm, abs_hbm, hour_hbm, dwell_hbm, addr_hbm,
    small_ref, expo_hbm,
    ps_ref, slot_ref, abs_ref, hour_ref, dwell_ref, addr_ref, expo_ref, even, odd, lines, lists, outb, recv, acc, label, sender, geo, weight, first, second, hots, out_a, in_a, out_b, in_b,
    in_sem, own_sem, out_sem, geo_sem, line_sem, list_sem, send_sem, line_in, list_in, recv_sem, msend_sem, nsend_sem, mrecv_sem,
):
    at, core = my_place()
    y, x, z = at
    inputs = ((ps_hbm, ps_ref), (slot_hbm, slot_ref), (abs_hbm, abs_ref), (hour_hbm, hour_ref), (dwell_hbm, dwell_ref), (addr_hbm, addr_ref))
    inputs = [pltpu.make_async_copy(a, b, in_sem.at[k]) for k, (a, b) in enumerate(inputs)]
    for copy in inputs:
        copy.start()
    own_lines = [pltpu.make_async_copy(em_hbm.at[pl.ds(p * PART, PART)], lines.at[p * 4], own_sem.at[p]) for p in range(3)]
    for copy in own_lines:
        copy.start()
    geo_copy = pltpu.make_async_copy(geo_hbm, geo, geo_sem)
    geo_copy.start()
    barrier = pltpu.get_barrier_semaphore()
    peers = 0
    for dy in range(4):
        for dx in range(4):
            for dz in range(4):
                for dc in range(2):
                    if 0 in (dy, dx, dz) and (dy, dx, dz, dc) != (0, 0, 0, 0):
                        to = ((y + dy) % 4) * 16 + ((x + dx) % 4) * 4 + (z + dz) % 4
                        pl.semaphore_signal(barrier, inc=1, device_id=(to, (core + dc) % 2), device_id_type=MESH)
                        peers += 1

    inputs[0].wait()
    entries = ps_ref[...].astype(F32)
    first[...] = jnp.concatenate([entries, entries], axis=0).T
    zero, one = first[pl.ds(0, 64, stride=2), :], first[pl.ds(1, 64, stride=2), :]
    left = lax.broadcasted_iota(I32, (64, 128), 1) < 64
    both, swapped = jnp.where(left, zero, one), jnp.where(left, one, zero)
    for a in range(4):
        for b in range(4):
            cut = slice((a * 4 + b) * 4, (a * 4 + b) * 4 + 4)
            even[a, b, :, 0, :] = both[cut]
            odd[a, b, :, 0, :] = swapped[cut]

    pl.semaphore_wait(barrier, peers)

    def plane_of(ref, p, where):
        return ref.at[where] if p == 0 else ref.at[:, where] if p == 1 else ref.at[:, :, where]

    for j in (1, 3, 2):
        for p in range(3):
            where = (at[p] + j) % 4
            to = sum(STRIDE[q] * (where if q == p else at[q]) for q in range(3))
            pltpu.make_async_remote_copy(
                src_ref=plane_of(odd if j % 2 else even, p, where), dst_ref=lists.at[p * 4 + j],
                send_sem=list_sem, recv_sem=list_in.at[p], device_id=(to, core), device_id_type=MESH,
            ).start()
            pltpu.make_async_remote_copy(
                src_ref=em_hbm.at[pl.ds(p * PART, PART)], dst_ref=lines.at[p * 4 + j],
                send_sem=line_sem, recv_sem=line_in.at[p], device_id=(to, core), device_id_type=MESH,
            ).start()
    for p in range(3):
        lists[p * 4] = plane_of(even, p, at[p])[...]
        own_lines[p].wait()
    for copy in inputs[1:]:
        copy.wait()

    def pick(u, p):
        b1, b2 = PLANE[p]
        line1 = [(at[b1] + u + 4 - v) % 4 for v in range(4)]
        line2 = [(at[b2] + v) % 4 for v in range(4)]

        @pl.when(u == 0)
        def _():
            drain(lists.at[pl.ds(p * 4 + 1, 3)], list_in.at[p])
            drain(lines.at[pl.ds(p * 4 + 1, 3)], line_in.at[p])

        found = []
        for i in range(4):
            row = jnp.concatenate([lists[p * 4 + i, line1[v], line2[v]] for v in range(4)], axis=1)
            upper = row >= 256.0
            table = one_hot(jnp.where(upper, row - 256.0, row).astype(I32), 256)
            source = lines[p * 4 + i]
            halves = jnp.concatenate([source[:, 0:256], source[:, 256:512]], axis=0)
            out = jnp.dot(halves, table, preferred_element_type=F32)
            found.append(jnp.where(upper, out[PART:], out[:PART]))
        low = lax.broadcasted_iota(I32, (PART, 512), 1) % 128 < 64
        for k in range(2):
            pairs = []
            for i in (0, 2):
                a, b = (found[i], found[i + 1]) if k == 0 else (found[i + 1], found[i])
                pairs.append(jnp.where(low, a, b).astype(BF16))
            for v in range(4):
                cut = slice(v * 128, (v + 1) * 128)
                outb[(p * 4 + u) * 8 + k * 4 + v] = jnp.concatenate([pairs[0][:, cut], pairs[1][:, cut]], axis=1)
        for dc in range(2):
            to_core = (core + dc) % 2
            for v in range(4):
                to = STRIDE[p] * at[p] + STRIDE[b1] * line1[v] + STRIDE[b2] * line2[v]
                copy = pltpu.make_async_remote_copy(
                    src_ref=outb.at[(p * 4 + u) * 8 + to_core * 4 + v], dst_ref=recv.at[(p * 4 + u) * 8 + dc * 4 + v],
                    send_sem=send_sem, recv_sem=recv_sem.at[p * 4 + u], device_id=(to, to_core), device_id_type=MESH,
                )
                if dc or v:
                    copy.start()
                else:

                    @pl.when(u > 0)
                    def _():
                        copy.start()

                    @pl.when(u == 0)
                    def _():
                        recv[p * 32] = outb[p * 32 + core * 4]

    slots = slot_ref[...]
    safe = jnp.maximum(slots, 0)
    source, entry = safe // CAP, safe % CAP
    apart = (
        (y + 4 - source // 32) % 4, (x + 4 - (source // 8) % 4) % 4, (z + 4 - (source // 2) % 4) % 4,
    )
    other = (core + 2 - source % 2) % 2
    for p in range(3):
        b1, b2 = PLANE[p]
        lane = (apart[p] // 2) * 128 + ((apart[p] + core) % 2) * 64 + entry
        group = jnp.where(slots >= 0, (apart[b1] + apart[b2]) % 4, -1)
        for g in range(4):
            label[p * 4 + g] = jnp.where(group == g, lane, -1)
        sender[p] = other * 4 + apart[b2]

    r = lax.broadcasted_iota(I32, (WIDTH, 128), 0)
    scale = jnp.zeros((WIDTH, 128), F32)
    for b in range(BANDS):
        scale = jnp.where(r // HOURS == b, jnp.float32(10.0 ** (A_WEIGHTING_DB[b] / 10.0)), scale)
    gain = jnp.zeros((WIDTH, 128), F32)
    for h in range(HOURS):
        period = hour_ref[h]
        g = jnp.where(period == 0, 1.0, jnp.where(period == 1, jnp.float32(10.0**0.5), jnp.where(period == 2, 10.0, 0.0)))
        gain = jnp.where(r % HOURS == h, g.astype(F32), gain)
    weight[...] = scale * gain / HOURS

    addr = permuted(
        addr_ref[...], lambda k: pl.ds(k // 2 * 32 + k % 2, 16, stride=2), lambda k: pl.ds(k * 16, 16), first, second
    )
    addr_high = jnp.maximum(addr, 0) // 128
    addr_low = jnp.where(addr >= 0, addr % 128, -1)
    for c in range(CAP_ADDR):
        hots[:, c * 128 : (c + 1) * 128] = one_hot(addr_low[c : c + 1], 128)
    acc[...] = jnp.zeros_like(acc)

    def gather(u, p):
        step = p * 4 + u

        @pl.when(u == 0)
        def _():
            drain(recv.at[pl.ds(p * 32 + 1, 7)], recv_sem.at[step])

        @pl.when(u > 0)
        def _():
            drain(recv.at[pl.ds(step * 8, 8)], recv_sem.at[step])

        def some_paths(n, inner):
            def row_of(ref, index):
                first_tile = n * (SPAN // PATHS_TILE)
                return jnp.concatenate([ref[index, pl.ds(first_tile + m, 1), :] for m in range(SPAN // PATHS_TILE)], axis=1)

            table = one_hot(row_of(label, step), 256)
            data = recv[pl.ds(step * 8, 8)].reshape(8 * PART, 256)
            out = jnp.dot(data, table, preferred_element_type=F32)
            which = row_of(sender, p)
            mine = out[0:PART]
            for k in range(1, 8):
                mine = jnp.where(which == k, out[k * PART : (k + 1) * PART], mine)
            cut = (slice(p * PART, (p + 1) * PART), pl.ds(pl.multiple_of(n * SPAN, SPAN), SPAN))
            acc[cut] = acc[cut] + mine
            return inner

        lax.fori_loop(0, PATHS // SPAN, some_paths, 0)

    def turn(u, carry):
        for p in range(3):

            @pl.when(u < 4)
            def _():
                pick(u, p)

            late = (p - AHEAD) % 3
            back = (AHEAD + late - p) // 3

            @pl.when((u >= back) & (u < 4 + back))
            def _():
                gather(u - back, late)

        return carry

    lax.fori_loop(0, 4 + (AHEAD + 2) // 3, turn, 0)
    geo_copy.wait()

    def tile(t, carry):
        gathered = acc[:, pl.ds(pl.multiple_of(t * PATHS_TILE, PATHS_TILE), PATHS_TILE)]
        damp = abs_ref[t].astype(F32)
        factor = jnp.concatenate(
            [jnp.broadcast_to(damp[b : b + 1], (HOURS, PATHS_TILE)) for b in range(BANDS)], axis=0
        )
        mixed = (factor * gathered).astype(BF16)
        exposure = lax.dot_general(mixed, geo[t], (((1,), (1,)), ((), ())), preferred_element_type=F32)
        expo_ref[:, pl.ds(pl.multiple_of(t * RECV_TILE, RECV_TILE), RECV_TILE)] = exposure
        for half in range(2):
            energy = jnp.sum(exposure[:, half * 128 : (half + 1) * 128] * weight[...], axis=0, keepdims=True)
            small_ref[pl.ds(2 * t + half, 1), :] = jnp.log(energy) * jnp.float32(1.0 / math.log(10.0))
        return carry

    lax.fori_loop(0, TILE_DEV, tile, 0)

    expo_copy = pltpu.make_async_copy(expo_ref, expo_hbm, out_sem)
    expo_copy.start()
    dwell = dwell_ref[...].astype(F32)
    table = jnp.concatenate([*split3(dwell * small_ref[0:16, :]), dwell.astype(BF16)], axis=0)
    found = jnp.dot(table, hots[...], preferred_element_type=F32)
    level_rows = found[0:16] + found[16:32] + found[32:48]
    weighted, dwelt = [], []
    for c in range(CAP_ADDR):
        lanes = slice(c * 128, (c + 1) * 128)
        mine = lax.broadcasted_iota(I32, (16, 128), 0) == addr_high[c : c + 1]
        weighted.append(jnp.sum(jnp.where(mine, level_rows[:, lanes], 0.0), axis=0, keepdims=True))
        dwelt.append(jnp.sum(jnp.where(mine, found[48:64, lanes], 0.0), axis=0, keepdims=True))
    out_a[...] = jnp.concatenate(weighted + dwelt + [jnp.zeros((96, 128), F32)], axis=0).T.reshape(8, 16, 128)
    mine_a, mine_b = y * 2 + core, x * 4 + z
    in_a[mine_a] = out_a[mine_a]
    for k in range(1, 8):
        to_y, to_core = (y + k // 2) % 4, (core + k % 2) % 2
        pltpu.make_async_remote_copy(
            src_ref=out_a.at[to_y * 2 + to_core], dst_ref=in_a.at[mine_a], send_sem=msend_sem, recv_sem=mrecv_sem.at[0],
            device_id=(to_y * 16 + mine_b, to_core), device_id_type=MESH,
        ).start()
    seven = in_a.at[pl.ds(0, 7)]
    pltpu.make_async_copy(seven, seven, mrecv_sem.at[0]).wait()
    for k in range(8):
        out_b[:, k, :] = in_a[k]
    in_b[mine_b] = out_b[mine_b]
    for k in range(1, 16):
        to = ((x + k // 4) % 4) * 4 + (z + k % 4) % 4
        pltpu.make_async_remote_copy(
            src_ref=out_b.at[to], dst_ref=in_b.at[mine_b], send_sem=nsend_sem, recv_sem=mrecv_sem.at[1],
            device_id=(y * 16 + to, core), device_id_type=MESH,
        ).start()
    fifteen = in_b.at[pl.ds(0, 15)]
    pltpu.make_async_copy(fifteen, fifteen, mrecv_sem.at[1]).wait()
    small_ref[16:144, :] = in_b[...].reshape(128, 128)

    drain(lists.at[pl.ds(0, 9)], list_sem)
    drain(lines.at[pl.ds(0, 9)], line_sem)
    drain(outb.at[pl.ds(0, 93)], send_sem)
    drain(out_a.at[pl.ds(0, 7)], msend_sem)
    drain(out_b.at[pl.ds(0, 15)], nsend_sem)
    expo_copy.wait()


def permuted(values, in_rows, out_rows, first, second):
    first[...] = jnp.concatenate([values.astype(F32), jnp.zeros((112, 128), F32)], axis=0).T
    for k in range(8):
        second[out_rows(k), :] = first[in_rows(k), :]
    return second[...].T[0:16].astype(I32)


def finish(small_ref, bld_ref, expo_in, level_ref, build_ref, expo_ref, passing, first, second, sems_in, sems_out):
    height = WIDTH // CUTS
    cuts = [pl.ds(k * height, height) for k in range(CUTS)]
    loads = [pltpu.make_async_copy(expo_in.at[c], passing.at[c], sems_in.at[k]) for k, c in enumerate(cuts)]
    stores = [pltpu.make_async_copy(passing.at[c], expo_ref.at[c], sems_out.at[k]) for k, c in enumerate(cuts)]
    for load in loads:
        load.start()
    for load, store in zip(loads, stores):
        load.wait()
        store.start()
    level_ref[...] = small_ref[0:16, :]
    got = small_ref[16:144, :].T
    bld = permuted(
        bld_ref[...], lambda k: pl.ds(k // 2 * 32 + k % 2, 16, stride=2), lambda k: pl.ds(k, 16, stride=8), first, second
    )
    bld_high, bld_low = bld // 128, bld % 128
    sub = lax.broadcasted_iota(I32, (128, 128), 0)
    lhs, hots = [], []
    for c in range(CAP_ADDR):
        mine = lax.broadcasted_iota(I32, (16, 128), 0) == bld_high[c : c + 1]
        spread = jnp.where(mine, got[c : c + 1], 0.0)
        count = jnp.where(mine, got[16 + c : 17 + c], 0.0)
        lhs.append(jnp.concatenate([*split3(spread), count.astype(BF16)], axis=0))
        hots.append(jnp.where(sub == bld_low[c : c + 1], 1.0, 0.0).astype(BF16))
    sums = lax.dot_general(
        jnp.concatenate(lhs, axis=1), jnp.concatenate(hots, axis=1), (((1,), (1,)), ((), ())), preferred_element_type=F32
    )
    build_ref[...] = (sums[0:16] + sums[16:32] + sums[32:48]) / jnp.maximum(sums[48:64], 1.0)
    for store in stores:
        store.wait()


def local(emission, path_sends, tile_slots, geometry, absorption, hour_period, dwellings, addr_sends, addr_building):
    vmem, hbm = pl.BlockSpec(memory_space=pltpu.VMEM), pl.BlockSpec(memory_space=pl.ANY)
    small, exposure = pl.pallas_call(
        kernel,
        out_shape=(
            jax.ShapeDtypeStruct((144, 128), F32),
            jax.ShapeDtypeStruct((WIDTH, TILE_DEV * RECV_TILE), F32),
        ),
        in_specs=[hbm] * 8,
        out_specs=(vmem, hbm),
        scratch_shapes=[
            pltpu.VMEM((CAP, DEVICES), I32),
            pltpu.VMEM((TILE_DEV, PATHS_TILE), I32),
            pltpu.VMEM((TILE_DEV, BANDS, PATHS_TILE), BF16),
            pltpu.SMEM((HOURS,), I32),
            pltpu.VMEM((16, 128), I32),
            pltpu.VMEM((CAP_ADDR, DEVICES), I32),
            pltpu.VMEM((WIDTH, TILE_DEV * RECV_TILE), F32),
            pltpu.VMEM((4, 4, 4, 1, 128), F32),
            pltpu.VMEM((4, 4, 4, 1, 128), F32),
            pltpu.VMEM((12, PART, SEG_DEV), BF16),
            pltpu.VMEM((12, 4, 4, 1, 128), F32),
            pltpu.VMEM((96, PART, 256), BF16),
            pltpu.VMEM((96, PART, 256), BF16),
            pltpu.VMEM((WIDTH, PATHS), F32),
            pltpu.VMEM((12, TILE_DEV, PATHS_TILE), I32),
            pltpu.VMEM((3, TILE_DEV, PATHS_TILE), I32),
            pltpu.VMEM((TILE_DEV, RECV_TILE, PATHS_TILE), BF16),
            pltpu.VMEM((WIDTH, 128), F32),
            pltpu.VMEM((128, 128), F32),
            pltpu.VMEM((128, 128), F32),
            pltpu.VMEM((128, 2048), BF16),
            pltpu.VMEM((8, 16, 128), F32),
            pltpu.VMEM((8, 16, 128), F32),
            pltpu.VMEM((16, 8, 128), F32),
            pltpu.VMEM((16, 8, 128), F32),
            pltpu.SemaphoreType.DMA((6,)),
            pltpu.SemaphoreType.DMA((3,)),
            pltpu.SemaphoreType.DMA,
            pltpu.SemaphoreType.DMA,
            pltpu.SemaphoreType.DMA,
            pltpu.SemaphoreType.DMA,
            pltpu.SemaphoreType.DMA,
            pltpu.SemaphoreType.DMA((3,)),
            pltpu.SemaphoreType.DMA((3,)),
            pltpu.SemaphoreType.DMA((12,)),
            pltpu.SemaphoreType.DMA,
            pltpu.SemaphoreType.DMA,
            pltpu.SemaphoreType.DMA((2,)),
        ],
        compiler_params=pltpu.CompilerParams(collective_id=0, has_side_effects=True, vmem_limit_bytes=60 * 2**20),
        name="noise_map",
    )(
        emission.T,
        path_sends[0].T,
        tile_slots,
        geometry,
        absorption,
        hour_period,
        dwellings.reshape(16, 128),
        addr_sends[0].T,
    )
    level, building, exposure = pl.pallas_call(
        finish,
        out_shape=(
            jax.ShapeDtypeStruct((16, 128), F32),
            jax.ShapeDtypeStruct((16, 128), F32),
            jax.ShapeDtypeStruct((WIDTH, TILE_DEV * RECV_TILE), F32),
        ),
        in_specs=[vmem, vmem, hbm],
        out_specs=(vmem, vmem, hbm),
        scratch_shapes=[
            pltpu.VMEM((WIDTH, TILE_DEV * RECV_TILE), F32),
            pltpu.VMEM((128, 128), F32),
            pltpu.VMEM((128, 128), F32),
            pltpu.SemaphoreType.DMA((CUTS,)),
            pltpu.SemaphoreType.DMA((CUTS,)),
        ],
        compiler_params=pltpu.CompilerParams(vmem_limit_bytes=60 * 2**20),
        name="buildings",
    )(small, addr_building[0].T, exposure)
    return level.reshape(-1), building.reshape(-1), exposure.T


def solution(mesh):
    both = ("region", "band")
    in_specs = (P(both, None), P(both, None, None), P(both, None), P(both, None, None), P(both, None, None), P(), P(both), P(both, None, None), P(both, None, None))
    out_specs = (P(both), P(both), P(both, None))
    return jax.shard_map(local, mesh=mesh, in_specs=in_specs, out_specs=out_specs, check_vma=False)
```

time: 71.2 us -> 63.7 us (0.89)
  Pallas kernels: 67.3 us -> 62.9 us
  local copies, waits for them, and re-layouts: 2.94 us -> 0 us
    pallas_call x1, Pallas kernels: 65.5 us -> 59.2 us  [local(): pl.pallas_call(kernel, out_shape=(jax.ShapeDtypeStruct((144, 128), F32),...]
    unnamed x8 -> x0, local copies, waits for them, and re-layouts: 2.94 us -> none
    pallas_call x1, Pallas kernels: 1.77 us -> 3.68 us  [local(): pl.pallas_call(finish, out_shape=(jax.ShapeDtypeStruct((16, 128), F32), j...]
where the time goes in v4:
time: 63.7 us; the launch traced here: 63.5 us
  Pallas kernels  62.9 us (99%)
  between operations  0.64 us (1%)
    pallas_call x1, Pallas kernels, local(): pl.pallas_call(kernel, out_shape=(jax.ShapeDtypeStruct((144, 128), F32),...  59.2 us
    pallas_call x1, Pallas kernels, local(): pl.pallas_call(finish, out_shape=(jax.ShapeDtypeStruct((16, 128), F32), j...  3.68 us

profile of v4, /device:TPU:1, one launch (start us, length us, event | category | flops | bytes accessed | tf_op | source)
XLA Modules:
  0.0 63.5 jit_solution(3389996869872793896)
XLA Ops:
  0.6 59.2 %noise_map.1 = (f32[144,128]{1,0:T(8,128)}, f32[192,2048]{1,0:T(8,128)}) custom-call(bf16[192,512]{1,0:T(8,128)(2,1)} %bitcast.14, s32[64,128]{1,0:T(8,128)} %bitcast.15, s32[8,512]{1,0:T(8,128)} %slot_hbm.1, bf16[8,256,512]{2,1,0:T(8,128)(2,1)} %geo_hbm.1, bf16[8,8,512]{2,1,0:T(8,128)(2,1)} %abs_hbm.1, s32[24]{0:T(128)} %hour_hbm.1, s32[16,128]{1,0:T(8,128)} %bitcast.16, ...), custom_call_target="tpu_custom_call" | custom-call | tf_op jit(solution)/shard_map/noise_map/pallas_call | solution.py:348
  59.9 3.7 %buildings.1 = (f32[16,128]{1,0:T(8,128)}, f32[16,128]{1,0:T(8,128)}, f32[192,2048]{1,0:T(8,128)}) custom-call(f32[144,128]{1,0:T(8,128)} %get-tuple-element.8.small_ref, s32[16,128]{1,0:T(8,128)} %bitcast.18, f32[192,2048]{1,0:T(8,128)} %get-tuple-element.9.expo_in), custom_call_target="tpu_custom_call" | custom-call | tf_op jit(solution)/shard_map/buildings/pallas_call | solution.py:408

commit v5 on v4

--- a/solution.py
+++ b/solution.py
@@ -258,7 +258,7 @@
             small_ref[pl.ds(2 * t + half, 1), :] = jnp.log(energy) * jnp.float32(1.0 / math.log(10.0))
         return carry
 
-    lax.fori_loop(0, TILE_DEV, tile, 0)
+    lax.fori_loop(0, TILE_DEV, tile, 0, unroll=4)
 
     expo_copy = pltpu.make_async_copy(expo_ref, expo_hbm, out_sem)
     expo_copy.start()

time: 63.7 us -> 62.7 us (0.984)
  Pallas kernels: 62.9 us -> 61.9 us
    pallas_call x1, Pallas kernels: 59.2 us -> 58.2 us  [local(): pl.pallas_call(kernel, out_shape=(jax.ShapeDtypeStruct((144, 128), F32),...]
where the time goes in v5:
time: 62.7 us; the launch traced here: 62.5 us
  Pallas kernels  61.9 us (99%)
  between operations  0.64 us (1%)
    pallas_call x1, Pallas kernels, local(): pl.pallas_call(kernel, out_shape=(jax.ShapeDtypeStruct((144, 128), F32),...  58.2 us
    pallas_call x1, Pallas kernels, local(): pl.pallas_call(finish, out_shape=(jax.ShapeDtypeStruct((16, 128), F32), j...  3.68 us

profile of v5, /device:TPU:1, one launch (start us, length us, event | category | flops | bytes accessed | tf_op | source)
XLA Modules:
  0.0 62.5 jit_solution(2926627446169725417)
XLA Ops:
  0.6 58.2 %noise_map.1 = (f32[144,128]{1,0:T(8,128)}, f32[192,2048]{1,0:T(8,128)}) custom-call(bf16[192,512]{1,0:T(8,128)(2,1)} %bitcast.14, s32[64,128]{1,0:T(8,128)} %bitcast.15, s32[8,512]{1,0:T(8,128)} %slot_hbm.1, bf16[8,256,512]{2,1,0:T(8,128)(2,1)} %geo_hbm.1, bf16[8,8,512]{2,1,0:T(8,128)(2,1)} %abs_hbm.1, s32[24]{0:T(128)} %hour_hbm.1, s32[16,128]{1,0:T(8,128)} %bitcast.16, ...), custom_call_target="tpu_custom_call" | custom-call | tf_op jit(solution)/shard_map/noise_map/pallas_call | solution.py:348
  58.8 3.7 %buildings.1 = (f32[16,128]{1,0:T(8,128)}, f32[16,128]{1,0:T(8,128)}, f32[192,2048]{1,0:T(8,128)}) custom-call(f32[144,128]{1,0:T(8,128)} %get-tuple-element.8.small_ref, s32[16,128]{1,0:T(8,128)} %bitcast.18, f32[192,2048]{1,0:T(8,128)} %get-tuple-element.9.expo_in), custom_call_target="tpu_custom_call" | custom-call | tf_op jit(solution)/shard_map/buildings/pallas_call | solution.py:408

commit v6 on v5

--- a/solution.py
+++ b/solution.py
@@ -22,7 +22,7 @@
 STRIDE = (16, 4, 1)
 PLANE = ((1, 2), (0, 2), (0, 1))
 SPAN = 4096
-CUTS = 6
+CUTS = 3
 AHEAD = 7
 A_WEIGHTING_DB = (-26.2, -16.1, -8.6, -3.2, 0.0, 1.2, 1.0, -1.1)
 MESH = pl.DeviceIdType.MESH
@@ -258,7 +258,7 @@
             small_ref[pl.ds(2 * t + half, 1), :] = jnp.log(energy) * jnp.float32(1.0 / math.log(10.0))
         return carry
 
-    lax.fori_loop(0, TILE_DEV, tile, 0, unroll=4)
+    lax.fori_loop(0, TILE_DEV, tile, 0, unroll=8)
 
     expo_copy = pltpu.make_async_copy(expo_ref, expo_hbm, out_sem)
     expo_copy.start()

time: 62.7 us -> 62.5 us (level)
  no operation moved by 1% of the time
where the time goes in v6:
time: 62.5 us; the launch traced here: 62.3 us
  Pallas kernels  61.7 us (99%)
  between operations  0.64 us (1%)
    pallas_call x1, Pallas kernels, local(): pl.pallas_call(kernel, out_shape=(jax.ShapeDtypeStruct((144, 128), F32),...  58 us
    pallas_call x1, Pallas kernels, local(): pl.pallas_call(finish, out_shape=(jax.ShapeDtypeStruct((16, 128), F32), j...  3.72 us

profile of v6, /device:TPU:1, one launch (start us, length us, event | category | flops | bytes accessed | tf_op | source)
XLA Modules:
  0.0 62.3 jit_solution(5176666244506532184)
XLA Ops:
  0.6 58.0 %noise_map.1 = (f32[144,128]{1,0:T(8,128)}, f32[192,2048]{1,0:T(8,128)}) custom-call(bf16[192,512]{1,0:T(8,128)(2,1)} %bitcast.14, s32[64,128]{1,0:T(8,128)} %bitcast.15, s32[8,512]{1,0:T(8,128)} %slot_hbm.1, bf16[8,256,512]{2,1,0:T(8,128)(2,1)} %geo_hbm.1, bf16[8,8,512]{2,1,0:T(8,128)(2,1)} %abs_hbm.1, s32[24]{0:T(128)} %hour_hbm.1, s32[16,128]{1,0:T(8,128)} %bitcast.16, ...), custom_call_target="tpu_custom_call" | custom-call | tf_op jit(solution)/shard_map/noise_map/pallas_call | solution.py:348
  58.6 3.7 %buildings.1 = (f32[16,128]{1,0:T(8,128)}, f32[16,128]{1,0:T(8,128)}, f32[192,2048]{1,0:T(8,128)}) custom-call(f32[144,128]{1,0:T(8,128)} %get-tuple-element.8.small_ref, s32[16,128]{1,0:T(8,128)} %bitcast.18, f32[192,2048]{1,0:T(8,128)} %get-tuple-element.9.expo_in), custom_call_target="tpu_custom_call" | custom-call | tf_op jit(solution)/shard_map/buildings/pallas_call | solution.py:408
